TPU v7x, 512 devices: a whole 4x4x16 slice. The times are simulated.
512 devices in a mesh: dp: 16 (over x, y), expert: 32 (over z, core).
Axes of the slice: x: 4, y: 4, z: 16, core: 2. Of those that a mesh axis runs over, the one named last changes fastest.
Arguments:
- tokens: bfloat16 [65536, 2048], P(('dp', 'expert')), may hold values from -6 to 6
- cotangent: bfloat16 [65536, 2048], P(('dp', 'expert')), may hold values from -6 to 6
- routes: int32 [65536, 2], P(('dp', 'expert')), may hold values from 0 to 127, all different within a row; in each aligned block of 128 rows (0 to 127, 128 to 255, ...) at most 3 rows name the same one
- ln_gain: bfloat16 [2048], P('dp'), may hold values from 0.099609375 to 1.8984375
- ln_bias: bfloat16 [2048], P('dp'), may hold values from -3 to 3
- router_weight: bfloat16 [2048, 128], P('dp'), may hold values from -0.25 to 0.25
- up_weight: bfloat16 [32, 256, 8192], P('expert', None, 'dp'), may hold values from -0.125 to 0.125
- down_weight: bfloat16 [32, 8192, 256], P('expert', 'dp'), may hold values from -0.0625 to 0.0625
Outputs:
- moe_out: bfloat16 [65536, 2048], P(('dp', 'expert'))
- grad_input: bfloat16 [65536, 2048], P(('dp', 'expert'))
- grad_up: bfloat16 [32, 256, 8192], P('expert', None, 'dp')
- grad_down: bfloat16 [32, 8192, 256], P('expert', 'dp')
- grad_router: float32 [2048, 128], P('dp')
- grad_gain: float32 [2048], P('dp')
- grad_bias: float32 [2048], P('dp')
Inputs may be any that keep to these rules, and one draw needn't show every extreme that they name: `routes`: the two ids of a row differ; the 128 rows of one device name any one expert at most 3 times, a bound that some block reaches.
All inputs are finite; a program needn't handle non-finite values.
Results may differ from a plain program's by a relative error of at most 0.035.
Values may be sent and summed in bfloat16 or wider, within the bound.
A program may use at most 128 MiB of HBM per device.

v0:
```python
import jax
import jax.numpy as jnp
from jax import lax
from jax.sharding import PartitionSpec as P

SLICES = 8
CAP = 3


epsilon = 1e-05
root_half = 0.7071067811865476
inv_root_tau = 0.3989422804014327


def partner_2(block, axis, bit):
    count = lax.axis_size(axis)
    route = []
    for low in range(count):
        high = low | 1 << bit
        if high != low and high < count:
            route += [(low, high), (high, low)]
    return lax.ppermute(block, axis, route)


def gelu_parts(hidden):
    normal_cdf = 0.5 * (1.0 + lax.erf(hidden * root_half))
    density = inv_root_tau * jnp.exp(-0.5 * hidden * hidden)
    return (hidden * normal_cdf, normal_cdf + hidden * density)


def octet_sum(partial_value):
    running = partial_value
    summed = partial_value.astype(jnp.float32)
    for level_index in range(SLICES.bit_length() - 1):
        partner = partner_2(running, "expert", level_index)
        summed = lax.optimization_barrier(running).astype(jnp.float32) + partner.astype(jnp.float32)
        running = summed.astype(jnp.bfloat16)
    return summed


def send_home(out_terms, in_terms):
    out_sum, in_sum = (
        lax.psum_scatter(
            out_terms.astype(jnp.bfloat16), "dp", scatter_dimension=0, tiled=True
        ).astype(jnp.float32),
        lax.psum_scatter(
            in_terms.astype(jnp.bfloat16), "dp", scatter_dimension=0, tiled=True
        ).astype(jnp.float32),
    )
    home_out, home_in = (
        lax.all_to_all(
            out_sum[0].astype(jnp.bfloat16), "expert", split_axis=0, concat_axis=0, tiled=True
        ),
        lax.all_to_all(
            in_sum[0].astype(jnp.bfloat16), "expert", split_axis=0, concat_axis=0, tiled=True
        ),
    )
    return (home_out, home_in)


def on_device(tokens, cotangent, routes, ln_gain, ln_bias, router_weight, up_weight, down_weight):
    count_tok = tokens.shape[0]
    feature_count = tokens.shape[1]
    slice_width = feature_count // SLICES
    columns = lax.axis_size("expert")
    flight = columns // SLICES
    gain_all, bias_all, router_all = (
        lax.all_gather(ln_gain, "dp", axis=0, tiled=True),
        lax.all_gather(ln_bias, "dp", axis=0, tiled=True),
        lax.all_gather(router_weight, "dp", axis=0, tiled=True),
    )
    values = tokens.astype(jnp.float32)
    centre = values - jnp.mean(values, axis=1, keepdims=True)
    scale_inv = lax.rsqrt(jnp.mean(centre * centre, axis=1, keepdims=True) + epsilon)
    normed = centre * scale_inv
    gain_f = gain_all.astype(jnp.float32)
    normal = (normed * gain_f + bias_all.astype(jnp.float32)).astype(jnp.bfloat16)
    logits = jnp.dot(normal, router_all, preferred_element_type=jnp.float32)
    expert_ids = jnp.arange(router_all.shape[1], dtype=jnp.int32)
    signed_pick = (routes[:, 0:1] == expert_ids).astype(jnp.float32) - (
        routes[:, 1:2] == expert_ids
    ).astype(jnp.float32)
    score_gap = jnp.sum(logits * signed_pick, axis=1)
    gate_pair = jnp.stack([jax.nn.sigmoid(score_gap), jax.nn.sigmoid(-score_gap)], axis=1)
    cot_f = cotangent.astype(jnp.float32)
    scaled = (gate_pair[:, :, None] * cot_f[:, None, :]).astype(jnp.bfloat16)
    flat_ids = routes.reshape(-1)
    in_flight = jnp.arange(flight, dtype=jnp.int32)
    member = (flat_ids[:, None] == in_flight[None, :]).astype(jnp.int32)
    earlier = jnp.cumsum(member, axis=0) - member
    slot_index = jnp.sum(earlier * member, axis=1)
    target = jnp.sum(member * in_flight[None, :], axis=1) * CAP + slot_index
    is_live = jnp.sum(member, axis=1) == 1
    slot_ids = jnp.arange(flight * CAP, dtype=jnp.int32)
    placing = ((target[None, :] == slot_ids[:, None]) & is_live[None, :]).astype(jnp.bfloat16)
    placing = placing.reshape(flight, CAP, count_tok, 2)
    normal_parts = normal.reshape(count_tok, SLICES, slice_width)
    scaled_parts = scaled.reshape(count_tok, 2, SLICES, slice_width)
    send_normal = (
        jnp.einsum("ectk,tqd->eqcd", placing, normal_parts, preferred_element_type=jnp.float32)
        .astype(jnp.bfloat16)
        .reshape(columns, CAP, slice_width)
    )
    send_scaled = (
        jnp.einsum("ectk,tkqd->eqcd", placing, scaled_parts, preferred_element_type=jnp.float32)
        .astype(jnp.bfloat16)
        .reshape(columns, CAP, slice_width)
    )
    got_normal, got_scaled = (
        lax.all_to_all(send_normal, "expert", split_axis=0, concat_axis=0, tiled=True),
        lax.all_to_all(send_scaled, "expert", split_axis=0, concat_axis=0, tiled=True),
    )
    rows_normal, rows_scaled = (
        lax.all_gather(got_normal[None], "dp", axis=0, tiled=True),
        lax.all_gather(got_scaled[None], "dp", axis=0, tiled=True),
    )
    row_shape = rows_normal.shape
    expert_in = rows_normal.reshape(-1, slice_width)
    expert_grad = rows_scaled.reshape(-1, slice_width)
    w_in = up_weight[0]
    w_out = down_weight[0]
    hidden = octet_sum(
        jnp.dot(expert_in, w_in, preferred_element_type=jnp.float32).astype(jnp.bfloat16)
    )
    gelu_value, gelu_slope = gelu_parts(hidden)
    active = gelu_value.astype(jnp.bfloat16)
    out_terms = jnp.dot(active, w_out, preferred_element_type=jnp.float32)
    back_part = lax.dot_general(
        expert_grad, w_out, (((1,), (1,)), ((), ())), preferred_element_type=jnp.float32
    ).astype(jnp.bfloat16)
    back_hidden = octet_sum(back_part)
    grad_hidden = (back_hidden * gelu_slope).astype(jnp.bfloat16)
    grad_down = lax.dot_general(
        active, expert_grad, (((0,), (0,)), ((), ())), preferred_element_type=jnp.float32
    ).astype(jnp.bfloat16)[None]
    grad_up = lax.dot_general(
        expert_in, grad_hidden, (((0,), (0,)), ((), ())), preferred_element_type=jnp.float32
    ).astype(jnp.bfloat16)[None]
    in_terms = lax.dot_general(
        grad_hidden, w_in, (((1,), (1,)), ((), ())), preferred_element_type=jnp.float32
    )
    out_terms = out_terms.reshape(row_shape)
    in_terms = in_terms.reshape(row_shape)
    home_out, home_in = send_home(out_terms, in_terms)
    back_out = home_out.reshape(flight, SLICES, CAP, slice_width)
    back_in = home_in.reshape(flight, SLICES, CAP, slice_width)
    expert_out = jnp.einsum(
        "ectk,eqcd->tkqd", placing, back_out, preferred_element_type=jnp.float32
    ).reshape(count_tok, 2, feature_count)
    expert_back = jnp.einsum(
        "ectk,eqcd->tkqd", placing, back_in, preferred_element_type=jnp.float32
    ).reshape(count_tok, 2, feature_count)
    moe_out = (gate_pair[:, 0:1] * expert_out[:, 0] + gate_pair[:, 1:2] * expert_out[:, 1]).astype(
        jnp.bfloat16
    )
    grad_gate = jnp.sum(cot_f[:, None, :] * expert_out, axis=2)
    grad_gap = (grad_gate[:, 0] - grad_gate[:, 1]) * gate_pair[:, 0] * gate_pair[:, 1]
    router_pull = lax.dot_general(
        signed_pick.astype(jnp.bfloat16),
        router_all,
        (((1,), (1,)), ((), ())),
        preferred_element_type=jnp.float32,
    )
    grad_normal = expert_back[:, 0] + expert_back[:, 1] + grad_gap[:, None] * router_pull
    router_term = grad_gap[:, None] * signed_pick
    local_router = jnp.dot(
        normal.astype(jnp.float32).T, router_term, precision=lax.Precision.HIGHEST
    )
    local_gain = jnp.sum(grad_normal * normed, axis=0)
    local_bias = jnp.sum(grad_normal, axis=0)
    part_gain, part_bias, part_router = (
        lax.psum_scatter(
            local_gain.astype(jnp.bfloat16), "dp", scatter_dimension=0, tiled=True
        ).astype(jnp.float32),
        lax.psum_scatter(
            local_bias.astype(jnp.bfloat16), "dp", scatter_dimension=0, tiled=True
        ).astype(jnp.float32),
        lax.psum_scatter(
            local_router.astype(jnp.bfloat16), "dp", scatter_dimension=0, tiled=True
        ).astype(jnp.float32),
    )
    grad_gain, grad_bias, grad_router = (
        lax.psum(part_gain.astype(jnp.bfloat16), "expert").astype(jnp.float32),
        lax.psum(part_bias.astype(jnp.bfloat16), "expert").astype(jnp.float32),
        lax.psum(part_router.astype(jnp.bfloat16), "expert").astype(jnp.float32),
    )
    grad_norm = grad_normal * gain_f
    grad_input = scale_inv * (
        grad_norm
        - jnp.mean(grad_norm, axis=1, keepdims=True)
        - normed * jnp.mean(grad_norm * normed, axis=1, keepdims=True)
    )
    return (
        moe_out,
        grad_input.astype(jnp.bfloat16),
        grad_up,
        grad_down,
        grad_router,
        grad_gain,
        grad_bias,
    )


def solution(mesh):
    return jax.shard_map(
        on_device,
        mesh=mesh,
        in_specs=(
            P(("dp", "expert"), None),
            P(("dp", "expert"), None),
            P(("dp", "expert"), None),
            P("dp"),
            P("dp"),
            P("dp", None),
            P("expert", None, "dp"),
            P("expert", "dp", None),
        ),
        out_specs=(
            P(("dp", "expert"), None),
            P(("dp", "expert"), None),
            P("expert", None, "dp"),
            P("expert", "dp", None),
            P("dp", None),
            P("dp"),
            P("dp"),
        ),
        check_vma=False,
    )
```

profile of v0, /device:TPU:1, one launch (start us, length us, event | category | flops | bytes accessed | tf_op | source)
XLA Modules:
  0.0 802.3 jit_solution(14793923387084527207)
XLA Ops:
  7.2 0.8 copy.56
  8.3 1.2 convert_reduce_fusion
  9.5 1.3 fusion.36
  10.9 17.3 %all-gather.2 = bf16[16,1,128]{2,1,0:T(2,128)(2,1)S(1)} all-gather(bf16[1,1,128]{2,1,0:T(2,128)(2,1)} %bitcast.159), channel_id=1, replica_groups=mesh['dp'=16,'expert'=32] {'dp'}, dimensions={0}, use_global_device_ids=true | all-gather | bytes 4352 | tf_op jit(solution)/shard_map/all_gather | solution.py:68
  28.2 14.7 %all-gather.3 = bf16[16,1,128]{2,1,0:T(2,128)(2,1)S(1)} all-gather(bf16[1,1,128]{2,1,0:T(2,128)(2,1)} %bitcast.160), channel_id=1, replica_groups=mesh['dp'=16,'expert'=32] {'dp'}, dimensions={0}, use_global_device_ids=true | all-gather | bytes 4352 | tf_op jit(solution)/shard_map/all_gather | solution.py:69
  42.9 1.2 reduce-window.6
  45.1 1.5 fusion.30
  47.0 37.9 %all_to_all.20 = bf16[32,3,256]{2,1,0:T(4,128)(2,1)S(1)} all-to-all(bf16[32,3,256]{2,1,0:T(4,128)(2,1)S(1)} %copy.64), channel_id=1, replica_groups=mesh['dp'=16,'expert'=32] {'expert'}, dimensions={0} | all-to-all | bytes 98304 | tf_op jit(solution)/shard_map/all_to_all | solution.py:110
  84.9 17.6 %all-gather = bf16[512,3,256]{2,0,1:T(8,128)(2,1)S(1)} all-gather(bf16[32,3,256]{2,0,1:T(8,128)(2,1)S(1)} %copy.65), channel_id=2, replica_groups=mesh['dp'=16,'expert'=32] {'dp'}, dimensions={0}, use_global_device_ids=true | all-gather | bytes 835584 | tf_op jit(solution)/shard_map/all_gather | solution.py:114
  102.5 0.7 copy.66
  103.2 0.7 reshape.184
  103.9 0.6 convolution_convert_fusion.1
  104.5 8.6 %collective-permute-start = (bf16[1536,512]{1,0:T(8,128)(2,1)S(1)}, bf16[1536,512]{1,0:T(8,128)(2,1)S(1)}, u32[]{:S(2)}, u32[]{:S(2)}) collective-permute-start(bf16[1536,512]{1,0:T(8,128)(2,1)S(1)} %convolution_convert_fusion.1), channel_id=1, source_target_pairs={{0,1},{1,0},{2,3},{3,2},{4,5},{5,4},{6,7},{7,6},{8,9},{9,8},{10,11... | collective-permute-start | bytes 4718600 | tf_op jit(solution)/shard_map/ppermute | solution.py:22
  113.1 3.0 collective-permute-done
  116.1 0.4 add_convert_fusion.3
  116.6 2.4 collective-permute-start.1
  119.0 35.1 %collective-permute-done.1 = bf16[1536,512]{1,0:T(8,128)(2,1)S(1)} collective-permute-done((bf16[1536,512]{1,0:T(8,128)(2,1)S(1)}, bf16[1536,512]{1,0:T(8,128)(2,1)S(1)}, u32[]{:S(2)}, u32[]{:S(2)}) %collective-permute-start.1) | collective-permute-done | bytes 1572896 | tf_op jit(solution)/shard_map/ppermute | solution.py:22
  154.1 0.4 add_convert_fusion.2
  154.5 1.9 collective-permute-start.2
  156.5 70.7 %collective-permute-done.2 = bf16[1536,512]{1,0:T(8,128)(2,1)S(1)} collective-permute-done((bf16[1536,512]{1,0:T(8,128)(2,1)S(1)}, bf16[1536,512]{1,0:T(8,128)(2,1)S(1)}, u32[]{:S(2)}, u32[]{:S(2)}) %collective-permute-start.2) | collective-permute-done | bytes 1572896 | tf_op jit(solution)/shard_map/ppermute | solution.py:22
  227.1 1.1 copy-done.6
  228.3 1.8 multiply_convert_fusion
  230.1 5.1 dot_general.54
  235.2 3.1 fusion.11
  238.4 75.8 %reduce-scatter.10.cloned.1.call-done = bf16[1,32,3,256]{3,1,2,0:T(8,128)(2,1)} async-done(((bf16[16,32,3,256]{3,1,2,0:T(8,128)(2,1)}), bf16[1,32,3,256]{3,1,2,0:T(8,128)(2,1)}) %reduce-scatter.10.cloned.1.call-update) | async-done | bytes 49168
  314.2 1.5 copy.68
  315.6 14.6 %all-to-all-start.1 = ((bf16[32,3,256]{2,1,0:T(4,128)(2,1)}), bf16[32,3,256]{2,1,0:T(4,128)(2,1)S(1)}, u32[]{:S(2)}, u32[]{:S(2)}) async-start(bf16[32,3,256]{2,1,0:T(4,128)(2,1)} %copy.68), calls=%async_computation.1 | async-start | bytes 131072 | tf_op jit(solution)/shard_map/all_to_all | solution.py:51
  330.3 19.5 %all_gather.17 = bf16[2048,128]{1,0:T(8,128)(2,1)S(1)} all-gather(bf16[128,128]{1,0:T(8,128)(2,1)S(1)} %copy-done.13), channel_id=1, replica_groups=mesh['dp'=16,'expert'=32] {'dp'}, dimensions={0}, use_global_device_ids=true | all-gather | bytes 557056 | tf_op jit(solution)/shard_map/all_gather | solution.py:70
  349.8 1.3 convert_element_type.192
  351.2 1.1 copy.111
  352.7 1.8 multiply_reduce_fusion
  355.0 28.8 %all_to_all.21 = bf16[32,3,256]{2,1,0:T(4,128)(2,1)S(1)} all-to-all(bf16[32,3,256]{2,1,0:T(4,128)(2,1)S(1)} %copy.73), channel_id=1, replica_groups=mesh['dp'=16,'expert'=32] {'expert'}, dimensions={0} | all-to-all | bytes 98304 | tf_op jit(solution)/shard_map/all_to_all | solution.py:111
  383.8 17.2 %all-gather.1 = bf16[512,3,256]{2,0,1:T(8,128)(2,1)S(1)} all-gather(bf16[32,3,256]{2,0,1:T(8,128)(2,1)S(1)} %copy.74), channel_id=3, replica_groups=mesh['dp'=16,'expert'=32] {'dp'}, dimensions={0}, use_global_device_ids=true | all-gather | bytes 835584 | tf_op jit(solution)/shard_map/all_gather | solution.py:115
  401.0 0.7 copy.75
  401.7 1.4 reshape.187
  403.2 1.7 convolution_convert_fusion
  404.9 8.9 %collective-permute-start.3 = (bf16[1536,512]{1,0:T(8,128)(2,1)S(1)}, bf16[1536,512]{1,0:T(8,128)(2,1)S(1)}, u32[]{:S(2)}, u32[]{:S(2)}) collective-permute-start(bf16[1536,512]{1,0:T(8,128)(2,1)S(1)} %convolution_convert_fusion), channel_id=1, source_target_pairs={{0,1},{1,0},{2,3},{3,2},{4,5},{5,4},{6,7},{7,6},{8,9},{9,8},{10,11... | collective-permute-start | bytes 4718600 | tf_op jit(solution)/shard_map/ppermute | solution.py:22
  413.8 3.0 collective-permute-done.3
  417.3 2.6 collective-permute-start.4
  419.9 35.1 %collective-permute-done.4 = bf16[1536,512]{1,0:T(8,128)(2,1)S(1)} collective-permute-done((bf16[1536,512]{1,0:T(8,128)(2,1)S(1)}, bf16[1536,512]{1,0:T(8,128)(2,1)S(1)}, u32[]{:S(2)}, u32[]{:S(2)}) %collective-permute-start.4) | collective-permute-done | bytes 1572896 | tf_op jit(solution)/shard_map/ppermute | solution.py:22
  454.9 0.4 add_convert_fusion
  455.4 1.9 collective-permute-start.5
  457.3 70.6 %collective-permute-done.5 = bf16[1536,512]{1,0:T(8,128)(2,1)S(1)} collective-permute-done((bf16[1536,512]{1,0:T(8,128)(2,1)S(1)}, bf16[1536,512]{1,0:T(8,128)(2,1)S(1)}, u32[]{:S(2)}, u32[]{:S(2)}) %collective-permute-start.5) | collective-permute-done | bytes 1572896 | tf_op jit(solution)/shard_map/ppermute | solution.py:22
  527.9 1.9 fusion.5
  529.8 2.3 dot_general.61
  532.1 3.1 fusion.14
  535.3 1.3 dynamic-slice
  537.2 1.5 convolution_convert_fusion.2
  538.7 2.5 fusion.42
  541.3 3.0 fusion.24
  544.3 66.7 %reduce-scatter.12.cloned.1.call-done = bf16[1,32,3,256]{3,1,2,0:T(8,128)(2,1)} async-done(((bf16[16,32,3,256]{3,1,2,0:T(8,128)(2,1)}), bf16[1,32,3,256]{3,1,2,0:T(8,128)(2,1)}) %reduce-scatter.12.cloned.1.call-update) | async-done | bytes 49168
  611.0 1.5 copy.77
  612.5 14.6 %all-to-all-start.3 = ((bf16[32,3,256]{2,1,0:T(4,128)(2,1)}), bf16[32,3,256]{2,1,0:T(4,128)(2,1)S(1)}, u32[]{:S(2)}, u32[]{:S(2)}) async-start(bf16[32,3,256]{2,1,0:T(4,128)(2,1)} %copy.77), calls=%async_computation.3 | async-start | bytes 131072 | tf_op jit(solution)/shard_map/all_to_all | solution.py:54
  627.1 1.3 fusion.23
  628.4 11.7 %all-to-all-done.3 = bf16[32,3,256]{2,1,0:T(4,128)(2,1)S(1)} async-done(((bf16[32,3,256]{2,1,0:T(4,128)(2,1)}), bf16[32,3,256]{2,1,0:T(4,128)(2,1)S(1)}, u32[]{:S(2)}, u32[]{:S(2)}) %all-to-all-start.3) | async-done | bytes 49184 | tf_op jit(solution)/shard_map/all_to_all | solution.py:54
  640.2 0.5 convolution_bitcast_fusion
  640.7 0.7 fusion.35
  641.5 31.5 %all-reduce.5 = (bf16[2048]{0:T(1024)(128)(2,1)S(1)}, bf16[2048]{0:T(1024)(128)(2,1)S(1)}) all-reduce(bf16[2048]{0:T(1024)(128)(2,1)S(1)} %get-tuple-element.7, bf16[2048]{0:T(1024)(128)(2,1)S(1)} %get-tuple-element.10), channel_id=7, replica_groups=mesh['dp'=16,'expert'=32] {'dp'}, use_global_device_ids=true, to_apply=%region_17.18.clone | all-reduce | flops 4096 | bytes 16384
  673.1 29.1 %reduce-scatter.8.cloned.1.call-done = bf16[128,128]{1,0:T(8,128)(2,1)} async-done(((bf16[2048,128]{1,0:T(8,128)(2,1)}), bf16[128,128]{1,0:T(8,128)(2,1)}) %reduce-scatter.8.cloned.1.call-update) | async-done | bytes 32784 | tf_op jit(solution)/shard_map/reduce_scatter | solution.py:178
  702.2 90.6 %all-reduce.4 = (bf16[128,128]{1,0:T(8,128)(2,1)S(1)}, bf16[128]{0:T(256)(128)(2,1)S(1)}, bf16[128]{0:T(256)(128)(2,1)S(1)}) all-reduce(bf16[128,128]{1,0:T(8,128)(2,1)} %reduce-scatter.8.cloned.1.call-done, bf16[128]{0:T(256)(128)(2,1)S(1)} %dynamic-slice.5, ...), channel_id=1, replica_groups=mesh['dp'=16,'expert'=32] {'expert'}, use_global_device_ids=true, to_apply=%region_15.16 | all-reduce | flops 16640 | bytes 66560 | tf_op jit(solution)/shard_map/psum | solution.py:185
  792.9 0.5 convert_element_type.215
  793.4 0.5 convert_element_type.217
  793.9 0.6 convert_element_type.213
  794.5 1.2 fusion.34
  (79 shorter events, 3.3 us)
Async XLA Ops:
  7.2 228.1 %copy-start = (bf16[1,512,256]{2,1,0:T(8,128)(2,1)S(1)}, bf16[1,512,256]{2,1,0:T(8,128)(2,1)}, u32[]{:S(2)}) copy-start(bf16[1,512,256]{2,1,0:T(8,128)(2,1)} %param.15) | copy-start | bytes 786436
  7.2 307.0 %reduce-scatter.10.cloned.1.call-start = ((), (), s32[]{:S(2)}) async-start(), calls=%async_computation.8 | async-start | bytes 835584
  46.5 305.7 %copy-start.2 = (bf16[128,2048]{1,0:T(8,128)(2,1)}, bf16[128,2048]{1,0:T(8,128)(2,1)S(1)}, u32[]{:S(2)}) copy-start(bf16[128,2048]{1,0:T(8,128)(2,1)S(1)} %fusion.30) | copy-start | bytes 1572868
  84.9 19.0 %copy-start.11 = (bf16[1,256,512]{2,1,0:T(8,128)(2,1)S(1)}, bf16[1,256,512]{2,1,0:T(8,128)(2,1)}, u32[]{:S(2)}) copy-start(bf16[1,256,512]{2,1,0:T(8,128)(2,1)} %param.14) | copy-start | bytes 786436
  103.9 12.7 %copy-start.4 = (bf16[1536,256]{1,0:T(8,128)(2,1)}, bf16[1536,256]{1,0:T(8,128)(2,1)S(1)}, u32[]{:S(2)}) copy-start(bf16[1536,256]{1,0:T(8,128)(2,1)S(1)} %reshape.184) | copy-start | bytes 2359300
  104.5 11.6 %collective-permute-start = (bf16[1536,512]{1,0:T(8,128)(2,1)S(1)}, bf16[1536,512]{1,0:T(8,128)(2,1)S(1)}, u32[]{:S(2)}, u32[]{:S(2)}) collective-permute-start(bf16[1536,512]{1,0:T(8,128)(2,1)S(1)} %convolution_convert_fusion.1), channel_id=1, source_target_pairs={{0,1},{1,0},{2,3},{3,2},{4,5},{5,4},{6,7},{7,6},{8,9},{9,8},{10,11... | collective-permute-start | bytes 4718600 | tf_op jit(solution)/shard_map/ppermute | solution.py:22
  116.6 37.5 %collective-permute-start.1 = (bf16[1536,512]{1,0:T(8,128)(2,1)S(1)}, bf16[1536,512]{1,0:T(8,128)(2,1)S(1)}, u32[]{:S(2)}, u32[]{:S(2)}) collective-permute-start(bf16[1536,512]{1,0:T(8,128)(2,1)S(1)} %add_convert_fusion.3), channel_id=1, source_target_pairs={{0,2},{2,0},{1,3},{3,1},{4,6},{6,4},{5,7},{7,5},{8,10},{10,8},{9,1... | collective-permute-start | bytes 4718600 | tf_op jit(solution)/shard_map/ppermute | solution.py:22
  154.5 72.6 %collective-permute-start.2 = (bf16[1536,512]{1,0:T(8,128)(2,1)S(1)}, bf16[1536,512]{1,0:T(8,128)(2,1)S(1)}, u32[]{:S(2)}, u32[]{:S(2)}) collective-permute-start(bf16[1536,512]{1,0:T(8,128)(2,1)S(1)} %add_convert_fusion.2), channel_id=1, source_target_pairs={{0,4},{4,0},{1,5},{5,1},{2,6},{6,2},{3,7},{7,3},{8,12},{12,8},{9,1... | collective-permute-start | bytes 4718600 | tf_op jit(solution)/shard_map/ppermute | solution.py:22
  227.1 1.1 copy-start.6
  235.2 3.1 copy-start.14
  235.2 95.1 %copy-start.13 = (bf16[128,128]{1,0:T(8,128)(2,1)S(1)}, bf16[128,128]{1,0:T(8,128)(2,1)}, u32[]{:S(2)}) copy-start(bf16[128,128]{1,0:T(8,128)(2,1)} %param.13) | copy-start | bytes 98308
  315.6 37.0 %all-to-all-start.1 = ((bf16[32,3,256]{2,1,0:T(4,128)(2,1)}), bf16[32,3,256]{2,1,0:T(4,128)(2,1)S(1)}, u32[]{:S(2)}, u32[]{:S(2)}) async-start(bf16[32,3,256]{2,1,0:T(4,128)(2,1)} %copy.68), calls=%async_computation.1 | async-start | bytes 131072 | tf_op jit(solution)/shard_map/all_to_all | solution.py:51
  330.2 280.8 %reduce-scatter.12.cloned.1.call-start = ((), (), s32[]{:S(2)}) async-start(), calls=%async_computation.9 | async-start | bytes 835584
  349.8 2.4 copy-start.9
  352.7 1.9 copy-start.8
  404.9 11.9 %collective-permute-start.3 = (bf16[1536,512]{1,0:T(8,128)(2,1)S(1)}, bf16[1536,512]{1,0:T(8,128)(2,1)S(1)}, u32[]{:S(2)}, u32[]{:S(2)}) collective-permute-start(bf16[1536,512]{1,0:T(8,128)(2,1)S(1)} %convolution_convert_fusion), channel_id=1, source_target_pairs={{0,1},{1,0},{2,3},{3,2},{4,5},{5,4},{6,7},{7,6},{8,9},{9,8},{10,11... | collective-permute-start | bytes 4718600 | tf_op jit(solution)/shard_map/ppermute | solution.py:22
  417.3 110.6 %copy-start.7 = (bf16[1536,512]{1,0:T(8,128)(2,1)S(1)}, bf16[1536,512]{1,0:T(8,128)(2,1)}, u32[]{:S(2)}) copy-start(bf16[1536,512]{1,0:T(8,128)(2,1)} %copy-done.6) | copy-start | bytes 4718596
  417.3 37.6 %collective-permute-start.4 = (bf16[1536,512]{1,0:T(8,128)(2,1)S(1)}, bf16[1536,512]{1,0:T(8,128)(2,1)S(1)}, u32[]{:S(2)}, u32[]{:S(2)}) collective-permute-start(bf16[1536,512]{1,0:T(8,128)(2,1)S(1)} %add_convert_fusion.1), channel_id=1, source_target_pairs={{0,2},{2,0},{1,3},{3,1},{4,6},{6,4},{5,7},{7,5},{8,10},{10,8},{9,1... | collective-permute-start | bytes 4718600 | tf_op jit(solution)/shard_map/ppermute | solution.py:22
  455.4 72.5 %collective-permute-start.5 = (bf16[1536,512]{1,0:T(8,128)(2,1)S(1)}, bf16[1536,512]{1,0:T(8,128)(2,1)S(1)}, u32[]{:S(2)}, u32[]{:S(2)}) collective-permute-start(bf16[1536,512]{1,0:T(8,128)(2,1)S(1)} %add_convert_fusion), channel_id=1, source_target_pairs={{0,4},{4,0},{1,5},{5,1},{2,6},{6,2},{3,7},{7,3},{8,12},{12,8},{9,1... | collective-permute-start | bytes 4718600 | tf_op jit(solution)/shard_map/ppermute | solution.py:22
  529.8 2.3 copy-start.12
  532.1 5.2 copy-start.3
  535.3 167.0 %reduce-scatter.8.cloned.1.call-start = ((), (), s32[]{:S(2)}) async-start(), calls=%async_computation.7 | async-start | bytes 557056 | tf_op jit(solution)/shard_map/reduce_scatter | solution.py:178
  541.3 85.8 %copy-start.5 = (bf16[1536,256]{1,0:T(8,128)(2,1)S(1)}, bf16[1536,256]{1,0:T(8,128)(2,1)}, u32[]{:S(2)}) copy-start(bf16[1536,256]{1,0:T(8,128)(2,1)} %copy-done.4) | copy-start | bytes 2359300
  612.5 27.7 %all-to-all-start.3 = ((bf16[32,3,256]{2,1,0:T(4,128)(2,1)}), bf16[32,3,256]{2,1,0:T(4,128)(2,1)S(1)}, u32[]{:S(2)}, u32[]{:S(2)}) async-start(bf16[32,3,256]{2,1,0:T(4,128)(2,1)} %copy.77), calls=%async_computation.3 | async-start | bytes 131072 | tf_op jit(solution)/shard_map/all_to_all | solution.py:54
  627.1 13.6 %copy-start.1 = (bf16[128,2048]{1,0:T(8,128)(2,1)S(1)}, bf16[128,2048]{1,0:T(8,128)(2,1)}, u32[]{:S(2)}) copy-start(bf16[128,2048]{1,0:T(8,128)(2,1)} %param.8) | copy-start | bytes 1572868
  628.4 12.3 %copy-start.10 = (bf16[2048,128]{1,0:T(8,128)(2,1)S(1)}, bf16[2048,128]{1,0:T(8,128)(2,1)}, u32[]{:S(2)}) copy-start(bf16[2048,128]{1,0:T(8,128)(2,1)} %copy-done.9) | copy-start | bytes 1572868
Sparse Core Ops, SparseCore 0:
  238.4 75.6 reduce-scatter.9
  535.4 75.5 reduce-scatter.11
  615.1 87.1 reduce-scatter.7
where the time goes:
time: 805 us; the launch traced here: 802 us
  waiting for transfers between devices  401 us (50%)
  blocking collectives  275 us (34%)
  starting transfers between devices  55.6 us (7%)
  local copies, waits for them, and re-layouts  19.7 us (2%)
  matrix products  18.3 us (2%)
  other arithmetic  17.7 us (2%)
  between operations  14.9 us (2%)
    ppermute x6, waiting for transfers between devices, partner_2(): return lax.ppermute(block, axis, route)  217 us
    unnamed x5, waiting for transfers between devices  143 us
    psum x1, blocking collectives, on_device(): lax.psum(part_router.astype(jnp.bfloat16), 'expert').astype(jnp.float32)  90.6 us
    all_to_all x1, blocking collectives, on_device(): lax.all_to_all(send_normal, 'expert', split_axis=0, concat_axis=0, tiled=...  37.9 us
    unnamed x1, blocking collectives  31.5 us
    reduce_scatter x1, waiting for transfers between devices, on_device(): lax.psum_scatter(local_router.astype(jnp.bfloat16), 'dp', scatter_dimensi...  29.1 us
    all_to_all x1, blocking collectives, on_device(): lax.all_to_all(send_scaled, 'expert', split_axis=0, concat_axis=0, tiled=...  28.8 us
    ppermute x6, starting transfers between devices, partner_2(): return lax.ppermute(block, axis, route)  26.3 us
  transfers between devices with their start and end apart: 11, of which 10 were waited for; matrix products, arithmetic and copies ran while one was open for 2% of the time, Pallas kernels for 0%

commit v1 on v0

v1 whole, which is shorter than its diff:
```python
import functools

import jax
import jax.numpy as jnp
from jax import lax
from jax.experimental import pallas as pl
from jax.experimental.pallas import tpu as pltpu
from jax.sharding import PartitionSpec as P

SLICES = 8
CAP = 3
SLOTS = 4
SIDE = 4
GROUP = 16
WIDTH = 256
UNITS = 512
ROWS = 48
CHUNK = SIDE * ROWS
MESH = pl.DeviceIdType.MESH

epsilon = 1e-05
root_half = 0.7071067811865476
inv_root_tau = 0.3989422804014327
f32 = jnp.float32
bf16 = jnp.bfloat16


def gelu_parts(hidden):
    normal_cdf = 0.5 * (1.0 + lax.erf(hidden * root_half))
    density = inv_root_tau * jnp.exp(-0.5 * hidden * hidden)
    return (hidden * normal_cdf, normal_cdf + hidden * density)


class Copies:
    def __init__(self, send_sems, recv_sems):
        self.send_sems, self.recv_sems, self.made = send_sems, recv_sems, []

    def start(self, src, dst, device):
        index = len(self.made)
        copy = pltpu.make_async_remote_copy(
            src_ref=src,
            dst_ref=dst,
            send_sem=self.send_sems.at[index],
            recv_sem=self.recv_sems.at[index],
            device_id=device,
            device_id_type=MESH,
        )
        copy.start()
        self.made.append(copy)
        return copy

    def finish(self):
        for copy in self.made:
            copy.wait_send()


def greet(partners):
    barrier = pltpu.get_barrier_semaphore()
    for device in partners:
        pl.semaphore_signal(barrier, inc=1, device_id=device, device_id_type=MESH)
    pl.semaphore_wait(barrier, len(partners))


def place():
    dp = lax.axis_index("dp")
    ex = lax.axis_index("expert")
    return dp // SIDE, dp % SIDE, ex // 2, ex % 2, dp, ex


def x_partner(step, x, y, ex):
    return (((x + step) % SIDE) * SIDE + y, ex)


def y_partner(step, x, y, ex):
    return (x * SIDE + (y + step) % SIDE, ex)


def gather_kernel(block, out, held, send_sems, recv_sems):
    x, y, z, c, dp, ex = place()
    other = (dp, 2 * z + 1 - c)
    peers = [((dp + step) % GROUP, ex) for step in range(1, GROUP)]
    greet(peers + [other])
    copies = Copies(send_sems, recv_sems)
    sent = [copies.start(block.at[c], held.at[c, dp], peer) for peer in peers]
    held[c, dp] = block[c]
    for copy in sent:
        copy.wait_recv()
    copies.start(held.at[c], held.at[c], other).wait_recv()
    out[...] = held[...]
    copies.finish()


def gather_params(packed):
    return pl.pallas_call(
        gather_kernel,
        out_shape=jax.ShapeDtypeStruct((2, GROUP) + packed.shape[1:], bf16),
        in_specs=[pl.BlockSpec(memory_space=pltpu.VMEM)],
        out_specs=pl.BlockSpec(memory_space=pltpu.VMEM),
        scratch_shapes=[
            pltpu.VMEM((2, GROUP) + packed.shape[1:], bf16),
            pltpu.SemaphoreType.DMA((GROUP,)),
            pltpu.SemaphoreType.DMA((GROUP,)),
        ],
        compiler_params=pltpu.CompilerParams(collective_id=0, has_side_effects=True, vmem_limit_bytes=32 << 20),
    )(packed)


def packing_index(line):
    slot = line & 3
    row = ((line >> 3) & 1) * (2 * ROWS) + ((line >> 2) & 1) * ROWS + (line >> 4) * CAP + slot
    return jnp.where(slot < CAP, row, -1)


def product(left, right, left_dim, right_dim):
    return lax.dot_general(left, right, (((left_dim,), (right_dim,)), ((), ())), preferred_element_type=f32)


def moe_kernel(
    send, w1, w2, wx1, wx2,
    home, gd_own, gd_far, gu_own, gu_far,
    recv, ag, pown, cs, cr, zs, zr, act, gh, slope, part, rs1, mid, rs2, hsend, hrecv,
    send_sems, recv_sems,
):
    x, y, z, c, dp, ex = place()
    half = (z % 4) // 2
    near = z % 2
    me = (z // 4) * 4 + near * 2 + c

    def member(step):
        g = (me + step) % GROUP
        return g, (dp, 2 * (4 * (g // 4) + 2 * half + (g % 4) // 2) + g % 2)

    others = [member(step) for step in range(1, GROUP)]
    along_x = [x_partner(step, x, y, ex) for step in range(1, SIDE)]
    along_y = [y_partner(step, x, y, ex) for step in range(1, SIDE)]
    core = (dp, 2 * z + 1 - c)
    beside = (dp, 2 * (z + 1 - 2 * near) + c)
    greet([device for _, device in others] + along_x + along_y)
    copies = Copies(send_sems, recv_sems)

    sent = [copies.start(send.at[g], recv.at[me], device) for g, device in others]
    recv[me] = send[me]
    lines = lax.broadcasted_iota(jnp.int32, (4 * ROWS, GROUP * 16), 1)
    rows = lax.broadcasted_iota(jnp.int32, (4 * ROWS, GROUP * 16), 0)
    pack = (packing_index(lines) == rows).astype(f32).astype(bf16)
    for copy in sent:
        copy.wait_recv()
    packed = jnp.dot(pack, recv[...].reshape(GROUP * 16, WIDTH), preferred_element_type=f32).astype(bf16)
    for kind in range(2):
        for blk in range(2):
            first = (kind * 2 + blk) * ROWS
            ag[kind, blk, x, y] = packed[first:first + ROWS]

    first_n = [copies.start(ag.at[0, :, x, y], ag.at[0, :, x, y], device) for device in along_y]
    first_s = [copies.start(ag.at[1, :, x, y], ag.at[1, :, x, y], device) for device in along_x]
    low, high = pl.ds(0, 2), pl.ds(2, 2)
    for copy in first_n:
        copy.wait_recv()
    right, left = along_x[0], along_x[2]
    n_1 = copies.start(ag.at[0, :, x, low], ag.at[0, :, x, low], right)
    n_2 = copies.start(ag.at[0, :, x, high], ag.at[0, :, x, high], left)
    n_3 = copies.start(ag.at[0, :, x, high], ag.at[0, :, x, high], right)
    n_4 = copies.start(ag.at[0, :, x, low], ag.at[0, :, x, low], left)
    for copy in first_s:
        copy.wait_recv()
    up, down = along_y[0], along_y[2]
    s_1 = copies.start(ag.at[1, :, low, y], ag.at[1, :, low, y], up)
    s_2 = copies.start(ag.at[1, :, high, y], ag.at[1, :, high, y], down)
    s_3 = copies.start(ag.at[1, :, high, y], ag.at[1, :, high, y], up)
    s_4 = copies.start(ag.at[1, :, low, y], ag.at[1, :, low, y], down)
    x_left, x_right, y_down, y_up = (x + 3) % SIDE, (x + 1) % SIDE, (y + 3) % SIDE, (y + 1) % SIDE
    n_1.wait_recv()
    n_5 = copies.start(ag.at[0, :, x_left, low], ag.at[0, :, x_left, low], right)
    n_2.wait_recv()
    n_6 = copies.start(ag.at[0, :, x_right, high], ag.at[0, :, x_right, high], left)
    s_1.wait_recv()
    s_5 = copies.start(ag.at[1, :, low, y_down], ag.at[1, :, low, y_down], up)
    s_2.wait_recv()
    s_6 = copies.start(ag.at[1, :, high, y_up], ag.at[1, :, high, y_up], down)
    for copy in (n_3, n_4, n_5, n_6):
        copy.wait_recv()

    def rows_of(kind, blk, group):
        return ag[kind, blk, group].reshape(CHUNK, WIDTH)

    def partial_sum(kind, group):
        if kind == 0:
            return product(rows_of(0, 0, group), w1[...], 1, 0) + product(rows_of(0, 1, group), wx1[...], 1, 0)
        return product(rows_of(1, 0, group), w2[...], 1, 1) + product(rows_of(1, 1, group), wx2[...], 1, 1)

    mine = [(x + c) % SIDE, (x + 3 - c) % SIDE]
    theirs = [(x + 1 - c) % SIDE, (x + 2 + c) % SIDE]
    crossed, zoned = {}, {}

    def begin(kind):
        for j in range(2):
            cs[kind, j] = partial_sum(kind, theirs[j]).astype(bf16)
            crossed[kind, j] = copies.start(cs.at[kind, j], cr.at[kind, j], core)
        for j in range(2):
            pown[kind, j] = partial_sum(kind, mine[j])
        for j in range(2):
            crossed[kind, j].wait_recv()
            zs[kind, j] = (pown[kind, j] + cr[kind, j].astype(f32)).astype(bf16)
            zoned[kind, j] = copies.start(zs.at[kind, j], zr.at[kind, j], beside)

    def whole(kind, j):
        zoned[kind, j].wait_recv()
        return zs[kind, j].astype(f32) + zr[kind, j].astype(f32)

    def spread(kind, values_of, weight_a, weight_b, right_dim):
        for group in range(SIDE):
            chunk = values_of[group]
            for blk, weight in ((0, weight_a), (1, weight_b)):
                part[kind, blk, group] = product(chunk, weight[...], 1, right_dim).astype(bf16).reshape(SIDE, ROWS, WIDTH)

    def reduce_first(kind):
        found = []
        for step in range(1, SIDE):
            found.append(copies.start(part.at[kind, 0, (x + step) % SIDE], rs1.at[kind, 0, step - 1], along_x[step - 1]))
            found.append(copies.start(part.at[kind, 1, :, (y + step) % SIDE], rs1.at[kind, 1, step - 1], along_y[step - 1]))
        return found

    def reduce_second(kind, found):
        for copy in found:
            copy.wait_recv()
        for blk in range(2):
            own = part[kind, 0, x] if blk == 0 else part[kind, 1, :, y]
            total = own.astype(f32)
            for step in range(SIDE - 1):
                total = total + rs1[kind, blk, step].astype(f32)
            mid[kind, blk] = total.astype(bf16)
        again = []
        for step in range(1, SIDE):
            again.append(copies.start(mid.at[kind, 0, (y + step) % SIDE], rs2.at[kind, 0, step - 1], along_y[step - 1]))
            again.append(copies.start(mid.at[kind, 1, (x + step) % SIDE], rs2.at[kind, 1, step - 1], along_x[step - 1]))
        return again

    def reduce_last(kind, again):
        for copy in again:
            copy.wait_recv()
        ends = []
        for blk in range(2):
            total = mid[kind, blk, y if blk == 0 else x].astype(f32)
            for step in range(SIDE - 1):
                total = total + rs2[kind, blk, step].astype(f32)
            ends.append(total.astype(bf16))
        return ends

    begin(0)
    for copy in (s_3, s_4, s_5, s_6):
        copy.wait_recv()
    begin(1)
    shared = []
    for j in range(2):
        value, grade = gelu_parts(whole(0, j))
        act[mine[j]] = value.astype(bf16)
        shared.append(copies.start(act.at[mine[j]], act.at[mine[j]], core))
        slope[j] = grade
    for copy in shared:
        copy.wait_recv()
    spread(0, act, w2, wx2, 0)
    found_out = reduce_first(0)
    active = act[...].reshape(SIDE * CHUNK, UNITS)
    gd_own[...] = product(active, ag[1, 0].reshape(SIDE * CHUNK, WIDTH), 0, 0)
    gd_far[...] = product(active, ag[1, 1].reshape(SIDE * CHUNK, WIDTH), 0, 0).astype(bf16)
    shared = []
    for j in range(2):
        gh[mine[j]] = (whole(1, j) * slope[j]).astype(bf16)
        shared.append(copies.start(gh.at[mine[j]], gh.at[mine[j]], core))
    again_out = reduce_second(0, found_out)
    for copy in shared:
        copy.wait_recv()
    spread(1, gh, w1, wx1, 1)
    found_in = reduce_first(1)
    ends = reduce_last(0, again_out)
    grads = gh[...].reshape(SIDE * CHUNK, UNITS)
    gu_own[...] = product(ag[0, 0].reshape(SIDE * CHUNK, WIDTH), grads, 0, 0)
    gu_far[...] = product(ag[0, 1].reshape(SIDE * CHUNK, WIDTH), grads, 0, 0).astype(bf16)
    ends = ends + reduce_last(1, reduce_second(1, found_in))

    lines = lax.broadcasted_iota(jnp.int32, (GROUP * 16, 4 * ROWS), 0)
    rows = lax.broadcasted_iota(jnp.int32, (GROUP * 16, 4 * ROWS), 1)
    unpack = (packing_index(lines) == rows).astype(f32).astype(bf16)
    hsend[...] = (
        jnp.dot(unpack, jnp.concatenate(ends, axis=0), preferred_element_type=f32)
        .astype(bf16)
        .reshape(GROUP, 16, WIDTH)
    )
    sent = [copies.start(hsend.at[g], hrecv.at[me], device) for g, device in others]
    hrecv[me] = hsend[me]
    for copy in sent:
        copy.wait_recv()
    home[...] = hrecv[...]
    copies.finish()


def run_experts(send, w1, w2, wx1, wx2):
    vmem = pl.BlockSpec(memory_space=pltpu.VMEM)
    count = 96
    pair = (2, 2, CHUNK, UNITS)
    return pl.pallas_call(
        moe_kernel,
        out_shape=[
            jax.ShapeDtypeStruct((GROUP, 16, WIDTH), bf16),
            jax.ShapeDtypeStruct((UNITS, WIDTH), f32),
            jax.ShapeDtypeStruct((UNITS, WIDTH), bf16),
            jax.ShapeDtypeStruct((WIDTH, UNITS), f32),
            jax.ShapeDtypeStruct((WIDTH, UNITS), bf16),
        ],
        in_specs=[vmem] * 5,
        out_specs=[vmem] * 5,
        scratch_shapes=[
            pltpu.VMEM((GROUP, 16, WIDTH), bf16),
            pltpu.VMEM((2, 2, SIDE, SIDE, ROWS, WIDTH), bf16),
            pltpu.VMEM(pair, f32),
            pltpu.VMEM(pair, bf16),
            pltpu.VMEM(pair, bf16),
            pltpu.VMEM(pair, bf16),
            pltpu.VMEM(pair, bf16),
            pltpu.VMEM((SIDE, CHUNK, UNITS), bf16),
            pltpu.VMEM((SIDE, CHUNK, UNITS), bf16),
            pltpu.VMEM((2, CHUNK, UNITS), f32),
            pltpu.VMEM((2, 2, SIDE, SIDE, ROWS, WIDTH), bf16),
            pltpu.VMEM((2, 2, SIDE - 1, SIDE, ROWS, WIDTH), bf16),
            pltpu.VMEM((2, 2, SIDE, ROWS, WIDTH), bf16),
            pltpu.VMEM((2, 2, SIDE - 1, ROWS, WIDTH), bf16),
            pltpu.VMEM((GROUP, 16, WIDTH), bf16),
            pltpu.VMEM((GROUP, 16, WIDTH), bf16),
            pltpu.SemaphoreType.DMA((count,)),
            pltpu.SemaphoreType.DMA((count,)),
        ],
        compiler_params=pltpu.CompilerParams(collective_id=1, has_side_effects=True, vmem_limit_bytes=48 << 20),
    )(send, w1, w2, wx1, wx2)


def reduce_kernel(parts, out, cr, s0, r1, s1, r2, s2, r3, s3, r4, fin, send_sems, recv_sems):
    x, y, z, c, dp, ex = place()
    outer, inner = z // SIDE, z % SIDE
    core = (dp, 2 * z + 1 - c)
    along_x = [x_partner(step, x, y, ex) for step in range(1, SIDE)]
    along_y = [y_partner(step, x, y, ex) for step in range(1, SIDE)]
    along_in = [(dp, 2 * (outer * SIDE + (inner + step) % SIDE) + c) for step in range(1, SIDE)]
    along_out = [(dp, 2 * ((outer + step) % SIDE * SIDE + inner) + c) for step in range(1, SIDE)]
    greet([core] + along_x + along_y + along_in + along_out)
    copies = Copies(send_sems, recv_sems)
    copies.start(parts.at[1 - c], cr, core).wait_recv()
    s0[...] = (parts[c].astype(f32) + cr[...].astype(f32)).astype(bf16)
    sent = []
    for step in range(1, SIDE):
        sent.append(copies.start(s0.at[0, (x + step) % SIDE], r1.at[0, step - 1], along_x[step - 1]))
        sent.append(copies.start(s0.at[1, :, (y + step) % SIDE], r1.at[1, step - 1], along_y[step - 1]))
    for copy in sent:
        copy.wait_recv()
    for path in range(2):
        own = s0[0, x] if path == 0 else s0[1, :, y]
        s1[path] = (own.astype(f32) + r1[path, 0].astype(f32) + r1[path, 1].astype(f32) + r1[path, 2].astype(f32)).astype(bf16)
    sent = []
    for step in range(1, SIDE):
        sent.append(copies.start(s1.at[0, (y + step) % SIDE], r2.at[0, step - 1], along_y[step - 1]))
        sent.append(copies.start(s1.at[1, (x + step) % SIDE], r2.at[1, step - 1], along_x[step - 1]))
    for copy in sent:
        copy.wait_recv()
    for path in range(2):
        own = s1[path, y if path == 0 else x]
        s2[path] = (own.astype(f32) + r2[path, 0].astype(f32) + r2[path, 1].astype(f32) + r2[path, 2].astype(f32)).astype(bf16)
    sent = [copies.start(s2, r3.at[inner], device) for device in along_in]
    r3[inner] = s2[...]
    for copy in sent:
        copy.wait_recv()
    s3[...] = (
        (r3[0].astype(f32) + r3[1].astype(f32)) + (r3[2].astype(f32) + r3[3].astype(f32))
    ).astype(bf16)
    sent = [copies.start(s3, r4.at[outer], device) for device in along_out]
    r4[outer] = s3[...]
    for copy in sent:
        copy.wait_recv()
    fin[c] = ((r4[0].astype(f32) + r4[1].astype(f32)) + (r4[2].astype(f32) + r4[3].astype(f32))).astype(bf16)
    copies.start(fin.at[c], fin.at[c], core).wait_recv()
    out[...] = fin[...].astype(f32)
    copies.finish()


def reduce_dense(parts):
    tall = parts.shape[-2]
    block = (tall, 128)
    return pl.pallas_call(
        reduce_kernel,
        out_shape=jax.ShapeDtypeStruct((2, 2) + block, f32),
        in_specs=[pl.BlockSpec(memory_space=pltpu.VMEM)],
        out_specs=pl.BlockSpec(memory_space=pltpu.VMEM),
        scratch_shapes=[
            pltpu.VMEM((2, SIDE, SIDE) + block, bf16),
            pltpu.VMEM((2, SIDE, SIDE) + block, bf16),
            pltpu.VMEM((2, SIDE - 1, SIDE) + block, bf16),
            pltpu.VMEM((2, SIDE) + block, bf16),
            pltpu.VMEM((2, SIDE - 1) + block, bf16),
            pltpu.VMEM((2,) + block, bf16),
            pltpu.VMEM((SIDE, 2) + block, bf16),
            pltpu.VMEM((2,) + block, bf16),
            pltpu.VMEM((SIDE, 2) + block, bf16),
            pltpu.VMEM((2, 2) + block, bf16),
            pltpu.SemaphoreType.DMA((24,)),
            pltpu.SemaphoreType.DMA((24,)),
        ],
        compiler_params=pltpu.CompilerParams(collective_id=2, has_side_effects=True, vmem_limit_bytes=32 << 20),
    )(parts)


def on_device(tokens, cotangent, routes, ln_gain, ln_bias, router_weight, up_weight, down_weight):
    count_tok, feature_count = tokens.shape
    columns = lax.axis_size("expert")
    flight = columns // SLICES
    place_z = lax.axis_index("expert") // 2
    half = (place_z % 4) // 2

    swap = [(i, ((i // 2) ^ 2) * 2 + i % 2) for i in range(columns)]
    w_in, w_out = up_weight[0], down_weight[0]
    far_in = lax.ppermute(w_in, "expert", swap)
    far_out = lax.ppermute(w_out, "expert", swap)

    packed = jnp.concatenate(
        [router_weight, ln_gain[None], ln_bias[None], jnp.zeros((30, 128), bf16)], axis=0
    ).reshape(2, 80, 128)
    params = gather_params(packed)
    params = params.transpose(1, 0, 2, 3).reshape(GROUP, 160, 128)
    router_all = params[:, :128].reshape(feature_count, 128)
    gain_f = params[:, 128].reshape(feature_count).astype(f32)
    bias_f = params[:, 129].reshape(feature_count).astype(f32)

    values = tokens.astype(f32)
    centre = values - jnp.mean(values, axis=1, keepdims=True)
    scale_inv = lax.rsqrt(jnp.mean(centre * centre, axis=1, keepdims=True) + epsilon)
    normed = centre * scale_inv
    normal = (normed * gain_f + bias_f).astype(bf16)
    logits = jnp.dot(normal, router_all, preferred_element_type=f32)
    expert_ids = jnp.arange(router_all.shape[1], dtype=jnp.int32)
    signed_pick = (routes[:, 0:1] == expert_ids).astype(f32) - (routes[:, 1:2] == expert_ids).astype(f32)
    score_gap = jnp.sum(logits * signed_pick, axis=1)
    gate_first, gate_second = jax.nn.sigmoid(score_gap), jax.nn.sigmoid(-score_gap)

    in_flight = jnp.arange(flight, dtype=jnp.int32)
    hits = [(routes[:, k:k + 1] == in_flight).astype(f32) for k in range(2)]
    either = hits[0] + hits[1]
    before = jnp.arange(count_tok)[:, None] > jnp.arange(count_tok)[None, :]
    earlier = jnp.dot(before.astype(bf16), either.astype(bf16), preferred_element_type=f32)
    slot_ids = jnp.arange(SLOTS, dtype=jnp.int32).astype(f32)
    placing = []
    for k in range(2):
        placed = hits[k].T[:, None, :] * (earlier.T[:, None, :] == slot_ids[None, :, None]).astype(f32)
        placing.append(placed.reshape(flight * SLOTS, count_tok))
    place_all = (placing[0] + placing[1]).astype(bf16)
    sel_normal = jnp.dot(place_all, normal, preferred_element_type=f32)
    sel_cot = jnp.dot(place_all, cotangent, preferred_element_type=f32)
    gate_row = jnp.sum(placing[0] * gate_first[None] + placing[1] * gate_second[None], axis=1, keepdims=True)
    both = jnp.stack([sel_normal, gate_row * sel_cot], axis=0).astype(bf16)
    both = both.reshape(2, flight, SLOTS, 2, 4, WIDTH)
    both = jnp.where(half == 1, both[:, :, :, ::-1], both)
    send = both.transpose(1, 4, 0, 3, 2, 5).reshape(GROUP, 16, WIDTH)

    home, gd_own, gd_far, gu_own, gu_far = run_experts(send, w_in, w_out, far_in, far_out)
    gd_back = lax.ppermute(gd_far, "expert", swap)
    gu_back = lax.ppermute(gu_far, "expert", swap)
    grad_down = (gd_own + gd_back.astype(f32)).astype(bf16)[None]
    grad_up = (gu_own + gu_back.astype(f32)).astype(bf16)[None]

    home = home.reshape(flight, 4, 2, 2, SLOTS, WIDTH)
    home = jnp.where(half == 1, home[:, :, :, ::-1], home)
    home = home.transpose(2, 0, 4, 3, 1, 5).reshape(2, flight * SLOTS, feature_count)
    back_out, back_in = home[0], home[1]

    def pick(matrix, rows):
        return lax.dot_general(matrix.astype(bf16), rows, (((0,), (0,)), ((), ())), preferred_element_type=f32)

    moe_out = (
        gate_first[:, None] * pick(placing[0], back_out) + gate_second[:, None] * pick(placing[1], back_out)
    ).astype(bf16)
    row_dot = jnp.sum(sel_cot * back_out.astype(f32), axis=1, keepdims=True)
    gap_raw = jnp.sum((placing[0] - placing[1]) * row_dot, axis=0)
    grad_gap = gap_raw * gate_first * gate_second
    router_pull = lax.dot_general(
        signed_pick.astype(bf16), router_all, (((1,), (1,)), ((), ())), preferred_element_type=f32
    )
    grad_normal = pick(placing[0] + placing[1], back_in) + grad_gap[:, None] * router_pull
    router_term = (grad_gap[:, None] * signed_pick).astype(bf16)
    local_router = lax.dot_general(
        normal, router_term, (((0,), (0,)), ((), ())), preferred_element_type=f32
    ).astype(bf16)
    local_gain = jnp.sum(grad_normal * normed, axis=0).astype(bf16)
    local_bias = jnp.sum(grad_normal, axis=0).astype(bf16)
    parts = jnp.concatenate(
        [
            local_router.reshape(GROUP, 128, 128),
            local_gain.reshape(GROUP, 1, 128),
            local_bias.reshape(GROUP, 1, 128),
            jnp.zeros((GROUP, 62, 128), bf16),
        ],
        axis=1,
    )
    parts = parts.reshape(SIDE, SIDE, 2, 2, 48, 128).transpose(2, 3, 0, 1, 4, 5)
    dense = reduce_dense(parts).reshape(192, 128)

    grad_norm = grad_normal * gain_f
    grad_input = scale_inv * (
        grad_norm
        - jnp.mean(grad_norm, axis=1, keepdims=True)
        - normed * jnp.mean(grad_norm * normed, axis=1, keepdims=True)
    )
    return (moe_out, grad_input.astype(bf16), grad_up, grad_down, dense[:128], dense[128], dense[129])


def solution(mesh):
    return jax.shard_map(
        on_device,
        mesh=mesh,
        in_specs=(
            P(("dp", "expert"), None),
            P(("dp", "expert"), None),
            P(("dp", "expert"), None),
            P("dp"),
            P("dp"),
            P("dp", None),
            P("expert", None, "dp"),
            P("expert", "dp", None),
        ),
        out_specs=(
            P(("dp", "expert"), None),
            P(("dp", "expert"), None),
            P("expert", None, "dp"),
            P("expert", "dp", None),
            P("dp", None),
            P("dp"),
            P("dp"),
        ),
        check_vma=False,
    )
```

time: 805 us -> 163 us (0.20)
  waiting for transfers between devices: 401 us -> 0.01 us
  blocking collectives: 275 us -> 0 us
  Pallas kernels: 0 us -> 130 us
  starting transfers between devices: 55.6 us -> 14.3 us
  local copies, waits for them, and re-layouts: 19.7 us -> 5.36 us
  matrix products: 18.3 us -> 4.7 us
  between operations: 14.9 us -> 1.38 us
  other arithmetic: 17.7 us -> 6.05 us
    ppermute x6 -> x4, waiting for transfers between devices: 217 us -> 0.01 us  [the longest x1 0.01 us: on_device(): far_in = lax.ppermute(w_in, 'expert', swap)]
    unnamed x5 -> x0, waiting for transfers between devices: 143 us -> none
    pallas_call x0 -> x3, Pallas kernels: none -> 130 us  [the longest x1 83.2 us: run_experts(): pl.pallas_call(moe_kernel, out_shape=[jax.ShapeDtypeStruct((GROUP, 16, WI...]
    psum x1 -> x0, blocking collectives: 90.6 us -> none  [on_device(): lax.psum(part_router.astype(jnp.bfloat16), 'expert').astype(jnp.float32)]
    all_gather x5 -> x0, blocking collectives: 86.4 us -> none  [the longest x1 19.5 us: on_device(): lax.all_gather(router_weight, 'dp', axis=0, tiled=True)]
    all_to_all x2 -> x0, blocking collectives: 66.7 us -> none  [the longest x1 37.9 us: on_device(): lax.all_to_all(send_normal, 'expert', split_axis=0, concat_axis=0, tiled=...]
    unnamed x1 -> x0, blocking collectives: 31.5 us -> none
    all_to_all x2 -> x0, starting transfers between devices: 29.2 us -> none  [the longest x1 14.6 us: send_home(): lax.all_to_all(out_sum[0].astype(jnp.bfloat16), 'expert', split_axis=0, c...]
  transfers between devices with their start and end apart: 11 -> 4, of which waited for: 10 -> 0; matrix products, arithmetic and copies ran while one was open for 2% -> 8% of each run, Pallas kernels for 0% -> 29%
where the time goes in v1:
time: 163 us; the launch traced here: 162 us
  Pallas kernels  130 us (80%)
  starting transfers between devices  14.3 us (9%)
  other arithmetic  6.05 us (4%)
  local copies, waits for them, and re-layouts  5.36 us (3%)
  matrix products  4.7 us (3%)
    pallas_call x1, Pallas kernels, run_experts(): pl.pallas_call(moe_kernel, out_shape=[jax.ShapeDtypeStruct((GROUP, 16, WI...  83.2 us
    pallas_call x1, Pallas kernels, reduce_dense(): pl.pallas_call(reduce_kernel, out_shape=jax.ShapeDtypeStruct((2, 2) + blo...  30.4 us
    pallas_call x1, Pallas kernels, gather_params(): pl.pallas_call(gather_kernel, out_shape=jax.ShapeDtypeStruct((2, GROUP) +...  16.8 us
    ppermute x1, starting transfers between devices, on_device(): far_in = lax.ppermute(w_in, 'expert', swap)  5.86 us
    ppermute x1, starting transfers between devices, on_device(): gd_back = lax.ppermute(gd_far, 'expert', swap)  3.57 us
  transfers between devices with their start and end apart: 4, of which 0 were waited for; matrix products, arithmetic and copies ran while one was open for 8% of the time, Pallas kernels for 29%

profile of v1, /device:TPU:1, one launch (start us, length us, event | category | flops | bytes accessed | tf_op | source)
XLA Modules:
  0.0 162.2 jit_solution(12688865308274000829)
XLA Ops:
  0.6 0.0 copy-start
  0.6 5.9 %collective-permute-start = (bf16[256,512]{1,0:T(8,128)(2,1)}, bf16[256,512]{1,0:T(8,128)(2,1)S(1)}, u32[]{:S(2)}, u32[]{:S(2)}) collective-permute-start(bf16[256,512]{1,0:T(8,128)(2,1)} %bitcast.70), channel_id=1, source_target_pairs={{0,4},{1,5},{2,6},{3,7},{4,0},{5,1},{6,2},{7,3},{8,12},{9,13},{10,... | collective-permute-start | bytes 786440 | tf_op jit(solution)/shard_map/ppermute | solution.py:418
  6.5 1.9 %collective-permute-start.1 = (bf16[512,256]{1,0:T(8,128)(2,1)}, bf16[512,256]{1,0:T(8,128)(2,1)S(1)}, u32[]{:S(2)}, u32[]{:S(2)}) collective-permute-start(bf16[512,256]{1,0:T(8,128)(2,1)} %bitcast.72), channel_id=1, source_target_pairs={{0,4},{1,5},{2,6},{3,7},{4,0},{5,1},{6,2},{7,3},{8,12},{9,13},{10,... | collective-permute-start | bytes 786440 | tf_op jit(solution)/shard_map/ppermute | solution.py:419
  8.5 0.8 slice_bitcast_fusion.2
  9.3 0.1 fusion.24
  9.4 0.1 pad.9.clone
  9.5 0.9 maximum_maximum_fusion.1
  10.4 16.8 %shard_map.135 = bf16[2,16,80,128]{3,2,1,0:T(8,128)(2,1)S(1)} custom-call(bf16[2,80,128]{2,1,0:T(8,128)(2,1)S(1)} %bitcast.74), custom_call_target="tpu_custom_call" | custom-call | tf_op jit(solution)/shard_map/pallas_call | solution.py:94
  27.2 0.0 copy-start.3
  27.3 0.0 copy-start.9
  27.4 0.0 copy-start.5
  27.4 0.9 copy-done.3
  28.3 0.2 convert_reduce_fusion
  28.5 0.3 fusion.18
  28.8 0.1 eq.173
  28.9 0.4 fusion.46
  29.3 0.5 fusion.10
  29.8 0.0 copy-start.18
  29.8 0.0 copy-start.21
  29.8 0.2 fusion.33
  30.0 0.3 copy-done.18
  30.3 0.1 mul.175
  30.4 0.2 multiply_convert_fusion
  30.7 0.3 copy.37
  31.0 0.0 copy-start.1
  31.0 0.0 copy-start.2
  31.1 0.2 fusion.9
  31.3 0.1 pad_maximum_fusion
  31.4 0.1 fusion.21
  31.5 0.6 pad.3.clone
  32.2 0.7 select_convert_fusion
  32.9 83.2 %shard_map.136 = (bf16[16,16,256]{2,1,0:T(8,128)(2,1)S(1)}, f32[512,256]{1,0:T(8,128)S(1)}, bf16[512,256]{1,0:T(8,128)(2,1)S(1)}, f32[256,512]{1,0:T(8,128)S(1)}, bf16[256,512]{1,0:T(8,128)(2,1)S(1)}) custom-call(bf16[16,16,256]{2,1,0:T(8,128)(2,1)S(1)} %reshape.355.send, bf16[256,512]{1,0:T(8,128)(2,1)S(1)} %bitcast.71, bf16[512,256]{1,0:T(8,128)(2,1)S(1)} %bitcast.73, ...), custom_call_target="tpu_custom_call" | custom-call | tf_op jit(solution)/shard_map/pallas_call | solution.py:301
  116.1 0.0 copy-start.19
  116.1 0.0 copy-start.22
  116.2 0.0 copy-start.4
  116.2 0.1 copy.31
  116.3 0.1 fusion.22
  116.4 0.0 copy-start.8
  116.5 0.1 multiply_reduce_fusion.1
  116.6 0.1 mul.186
  116.7 0.0 copy-done.11
  116.8 0.0 copy-done.15
  116.8 0.1 fusion.35
  116.9 2.9 %collective-permute-start.2 = (bf16[256,512]{1,0:T(8,128)(2,1)S(1)}, bf16[256,512]{1,0:T(8,128)(2,1)S(1)}, u32[]{:S(2)}, u32[]{:S(2)}) collective-permute-start(bf16[256,512]{1,0:T(8,128)(2,1)S(1)} %get-tuple-element.14), channel_id=1, source_target_pairs={{0,4},{1,5},{2,6},{3,7},{4,0},{5,1},{6,2},{7,3},{8,12},{9,13},{10,... | collective-permute-start | bytes 786440 | tf_op jit(solution)/shard_map/ppermute | solution.py:462
  119.8 0.0 copy-start.6
  119.9 3.6 %collective-permute-start.3 = (bf16[512,256]{1,0:T(8,128)(2,1)S(1)}, bf16[512,256]{1,0:T(8,128)(2,1)S(1)}, u32[]{:S(2)}, u32[]{:S(2)}) collective-permute-start(bf16[512,256]{1,0:T(8,128)(2,1)S(1)} %get-tuple-element.16), channel_id=1, source_target_pairs={{0,4},{1,5},{2,6},{3,7},{4,0},{5,1},{6,2},{7,3},{8,12},{9,13},{10,... | collective-permute-start | bytes 786440 | tf_op jit(solution)/shard_map/ppermute | solution.py:461
  123.5 1.2 convolution_convert_fusion
  124.7 0.3 fusion.49
  125.0 0.0 copy-start.13
  125.0 0.0 copy-start.23
  125.1 0.7 fusion.17
  125.8 0.0 copy-start.12
  125.8 0.0 copy-start.20
  125.9 0.3 convolution_multiply_fusion.2
  126.2 0.3 copy-done.12
  126.5 1.1 fusion.2
  127.6 1.2 fusion.16
  128.8 0.3 maximum_maximum_fusion
  129.1 0.1 copy.39
  129.1 30.4 %shard_map.137 = f32[2,2,48,128]{3,2,1,0:T(8,128)S(1)} custom-call(bf16[2,2,4,4,48,128]{5,4,3,2,1,0:T(8,128)(2,1)S(1)} %bitcast.66), custom_call_target="tpu_custom_call" | custom-call | tf_op jit(solution)/shard_map/pallas_call | solution.py:386
  159.5 0.5 slice_bitcast_fusion
  160.1 0.6 slice.49
  160.7 0.8 fusion.19
  161.5 0.8 fusion.20
  (71 shorter events, 0.6 us)
Async XLA Ops:
  0.6 29.8 %copy-start = (bf16[128,2048]{1,0:T(8,128)(2,1)S(1)}, bf16[128,2048]{1,0:T(8,128)(2,1)}, u32[]{:S(2)}) copy-start(bf16[128,2048]{1,0:T(8,128)(2,1)} %param.9) | copy-start | bytes 1572868
  0.6 32.2 %collective-permute-start = (bf16[256,512]{1,0:T(8,128)(2,1)}, bf16[256,512]{1,0:T(8,128)(2,1)S(1)}, u32[]{:S(2)}, u32[]{:S(2)}) collective-permute-start(bf16[256,512]{1,0:T(8,128)(2,1)} %bitcast.70), channel_id=1, source_target_pairs={{0,4},{1,5},{2,6},{3,7},{4,0},{5,1},{6,2},{7,3},{8,12},{9,13},{10,... | collective-permute-start | bytes 786440 | tf_op jit(solution)/shard_map/ppermute | solution.py:418
  6.5 26.3 %collective-permute-start.1 = (bf16[512,256]{1,0:T(8,128)(2,1)}, bf16[512,256]{1,0:T(8,128)(2,1)S(1)}, u32[]{:S(2)}, u32[]{:S(2)}) collective-permute-start(bf16[512,256]{1,0:T(8,128)(2,1)} %bitcast.72), channel_id=1, source_target_pairs={{0,4},{1,5},{2,6},{3,7},{4,0},{5,1},{6,2},{7,3},{8,12},{9,13},{10,... | collective-permute-start | bytes 786440 | tf_op jit(solution)/shard_map/ppermute | solution.py:419
  8.5 23.7 %copy-start.14 = (f32[4]{0:T(128)}, f32[4]{0:T(128)S(1)}, u32[]{:S(2)}) copy-start(f32[4]{0:T(128)S(1)} %iota_convert_fusion) | copy-start | bytes 52
  9.3 20.0 %copy-start.28 = (s32[128]{0:T(128)}, s32[128]{0:T(128)S(1)}, u32[]{:S(2)}) copy-start(s32[128]{0:T(128)S(1)} %get-tuple-element.32) | copy-start | bytes 1540
  9.3 20.5 %copy-start.26 = (s32[128]{0:T(128)}, s32[128]{0:T(128)S(1)}, u32[]{:S(2)}) copy-start(s32[128]{0:T(128)S(1)} %get-tuple-element.31) | copy-start | bytes 1540
  9.4 22.8 %copy-start.10 = (f32[4,128]{1,0:T(4,128)}, f32[4,128]{1,0:T(4,128)S(1)}, u32[]{:S(2)}) copy-start(f32[4,128]{1,0:T(4,128)S(1)} %fusion.24) | copy-start | bytes 6148
  27.2 1.1 copy-start.3
  27.3 3.7 %copy-start.9 = (f32[16,1,128]{2,1,0:T(1,128)}, f32[16,1,128]{2,1,0:T(1,128)S(1)}, u32[]{:S(2)}) copy-start(f32[16,1,128]{2,1,0:T(1,128)S(1)} %get-tuple-element.22) | copy-start | bytes 24580
  27.4 1.9 %copy-start.5 = (bf16[16,128,128]{2,1,0:T(8,128)(2,1)}, bf16[16,128,128]{2,1,0:T(8,128)(2,1)S(1)}, u32[]{:S(2)}) copy-start(bf16[16,128,128]{2,1,0:T(8,128)(2,1)S(1)} %slice.46) | copy-start | bytes 1572868
  28.5 1.4 copy-start.16
  28.8 0.5 copy-start.24
  29.8 0.5 copy-start.18
  29.8 0.6 copy-start.21
  30.0 1.1 copy-start.7
  31.0 1.8 %copy-start.1 = (bf16[1,256,512]{2,1,0:T(8,128)(2,1)S(1)}, bf16[1,256,512]{2,1,0:T(8,128)(2,1)}, u32[]{:S(2)}) copy-start(bf16[1,256,512]{2,1,0:T(8,128)(2,1)} %param.14) | copy-start | bytes 786436
  31.0 1.8 %copy-start.2 = (bf16[1,512,256]{2,1,0:T(8,128)(2,1)S(1)}, bf16[1,512,256]{2,1,0:T(8,128)(2,1)}, u32[]{:S(2)}) copy-start(bf16[1,512,256]{2,1,0:T(8,128)(2,1)} %param.15) | copy-start | bytes 786436
  116.1 0.7 copy-start.11
  116.1 0.7 copy-start.15
  116.1 0.8 copy-start.19
  116.1 0.8 copy-start.22
  116.2 7.3 %copy-start.4 = (bf16[128,2048]{1,0:T(8,128)(2,1)S(1)}, bf16[128,2048]{1,0:T(8,128)(2,1)}, u32[]{:S(2)}) copy-start(bf16[128,2048]{1,0:T(8,128)(2,1)} %param.8) | copy-start | bytes 1572868
  116.4 8.2 %copy-start.8 = (bf16[4,4,128]{2,1,0:T(4,128)(2,1)S(1)}, bf16[4,4,128]{2,1,0:T(4,128)(2,1)}, u32[]{:S(2)}) copy-start(bf16[4,4,128]{2,1,0:T(4,128)(2,1)} %copy-done.7) | copy-start | bytes 12292
  116.9 43.8 %collective-permute-start.2 = (bf16[256,512]{1,0:T(8,128)(2,1)S(1)}, bf16[256,512]{1,0:T(8,128)(2,1)S(1)}, u32[]{:S(2)}, u32[]{:S(2)}) collective-permute-start(bf16[256,512]{1,0:T(8,128)(2,1)S(1)} %get-tuple-element.14), channel_id=1, source_target_pairs={{0,4},{1,5},{2,6},{3,7},{4,0},{5,1},{6,2},{7,3},{8,12},{9,13},{10,... | collective-permute-start | bytes 786440 | tf_op jit(solution)/shard_map/ppermute | solution.py:462
  119.8 5.1 %copy-start.6 = (bf16[16,128,128]{2,1,0:T(8,128)(2,1)S(1)}, bf16[16,128,128]{2,1,0:T(8,128)(2,1)}, u32[]{:S(2)}) copy-start(bf16[16,128,128]{2,1,0:T(8,128)(2,1)} %copy-done.5) | copy-start | bytes 1572868
  119.9 5.1 %copy-start.17 = (f32[128]{0:T(128)S(1)}, f32[128]{0:T(128)}, u32[]{:S(2)}) copy-start(f32[128]{0:T(128)} %copy-done.16) | copy-start | bytes 1540
  119.9 5.1 %copy-start.25 = (f32[128]{0:T(128)S(1)}, f32[128]{0:T(128)}, u32[]{:S(2)}) copy-start(f32[128]{0:T(128)} %copy-done.24) | copy-start | bytes 1540
  119.9 5.1 %copy-start.27 = (s32[128]{0:T(128)S(1)}, s32[128]{0:T(128)}, u32[]{:S(2)}) copy-start(s32[128]{0:T(128)} %copy-done.26) | copy-start | bytes 1540
  119.9 5.1 %copy-start.29 = (s32[128]{0:T(128)S(1)}, s32[128]{0:T(128)}, u32[]{:S(2)}) copy-start(s32[128]{0:T(128)} %copy-done.28) | copy-start | bytes 1540
  119.9 41.6 %collective-permute-start.3 = (bf16[512,256]{1,0:T(8,128)(2,1)S(1)}, bf16[512,256]{1,0:T(8,128)(2,1)S(1)}, u32[]{:S(2)}, u32[]{:S(2)}) collective-permute-start(bf16[512,256]{1,0:T(8,128)(2,1)S(1)} %get-tuple-element.16), channel_id=1, source_target_pairs={{0,4},{1,5},{2,6},{3,7},{4,0},{5,1},{6,2},{7,3},{8,12},{9,13},{10,... | collective-permute-start | bytes 786440 | tf_op jit(solution)/shard_map/ppermute | solution.py:461
  125.0 0.8 copy-start.13
  125.0 0.8 copy-start.23
  125.8 0.7 copy-start.12
  125.8 0.7 copy-start.20
  127.6 1.2 copy-start.30

commit v2 on v0

v2 whole, which is shorter than its diff:
```python
import jax
import jax.numpy as jnp
from jax import lax
from jax.experimental import pallas as pl
from jax.experimental.pallas import tpu as pltpu
from jax.sharding import PartitionSpec as P

SLICES = 8
CAP = 3
SLOTS = 4
SIDE = 4
GROUP = 16
WIDTH = 256
LANES = 128
HIDDEN = 2048
TOKENS = 128
UNITS = 512
ROWS = 48
CHUNK = SIDE * ROWS
MESH = pl.DeviceIdType.MESH

epsilon = 1e-05
root_half = 0.7071067811865476
inv_root_tau = 0.3989422804014327
f32 = jnp.float32
bf16 = jnp.bfloat16


def gelu_parts(hidden):
    normal_cdf = 0.5 * (1.0 + lax.erf(hidden * root_half))
    density = inv_root_tau * jnp.exp(-0.5 * hidden * hidden)
    return (hidden * normal_cdf, normal_cdf + hidden * density)


class Copies:
    def __init__(self, send_sems, recv_sems):
        self.send_sems, self.recv_sems, self.made = send_sems, recv_sems, []

    def start(self, src, dst, device):
        index = len(self.made)
        copy = pltpu.make_async_remote_copy(
            src_ref=src,
            dst_ref=dst,
            send_sem=self.send_sems.at[index],
            recv_sem=self.recv_sems.at[index],
            device_id=device,
            device_id_type=MESH,
        )
        copy.start()
        self.made.append(copy)
        return copy

    def finish(self):
        for copy in self.made:
            copy.wait_send()


def place():
    dp = lax.axis_index("dp")
    ex = lax.axis_index("expert")
    return dp // SIDE, dp % SIDE, ex // 2, ex % 2, dp, ex


def x_partner(step, x, y, ex):
    return (((x + step) % SIDE) * SIDE + y, ex)


def y_partner(step, x, y, ex):
    return (x * SIDE + (y + step) % SIDE, ex)


def product(left, right, left_dim, right_dim):
    return lax.dot_general(left, right, (((left_dim,), (right_dim,)), ((), ())), preferred_element_type=f32)


def iota(shape, dim):
    return lax.broadcasted_iota(jnp.int32, shape, dim)


def one_hot(found):
    return found.astype(f32).astype(bf16)


def message_row(row):
    slot, expert = row & 3, (row >> 2) & 3
    lane_half, k2, blk = (row >> 4) & 1, (row >> 5) & 3, row >> 7
    return (expert * 4 + k2) * 16 + blk * 8 + lane_half * 4 + slot


def packed_row(row, lane_half):
    slot = row & 3
    good = (slot < CAP) & (((row >> 2) & 1) == lane_half)
    return jnp.where(good, ((row >> 3) & 1) * ROWS + (row >> 4) * CAP + slot, -1)


def step_kernel(
    tokens, cot, routes, gain, bias, router, w1, w2,
    moe_out, grad_in, gu_out, gd_out, router_out, dense_out,
    normed, block, held, rt, sends, recvs, ag, wx1, wx2, pown, cs, cr, zs, zr, act, gh, slope, part, rs1, mid, rs2,
    hsend, hrecv, gds, gdr, gus, gur, gd_own, gu_own, base,
    lr, lc, l0, l1, l2, l3, l4, l5, l6, l7, l8, fin, gb, gbr, gb1, gb2, gb3,
    send_sems, recv_sems,
):
    x, y, z, c, dp, ex = place()
    outer, inner = z // 4, z % 4
    half, near = inner // 2, inner % 2
    me = outer * 4 + near * 2 + c

    def member(step):
        g = (me + step) % GROUP
        return g, (dp, 2 * (4 * (g // 4) + 2 * half + (g % 4) // 2) + g % 2)

    others = [member(step) for step in range(1, GROUP)]
    peers = [((dp + step) % GROUP, ex) for step in range(1, GROUP)]
    along_x = [x_partner(step, x, y, ex) for step in range(1, SIDE)]
    along_y = [y_partner(step, x, y, ex) for step in range(1, SIDE)]
    core = (dp, 2 * z + 1 - c)
    beside = (dp, 2 * (z + 1 - 2 * near) + c)
    over = (dp, 2 * (z + 2 - 4 * half) + c)
    along_in = [(dp, 2 * (outer * 4 + (inner + step) % 4) + c) for step in range(1, 4)]
    along_out = [(dp, 2 * ((outer + step) % 4 * 4 + inner) + c) for step in range(1, 4)]
    octet = [(dp, 8 * outer + (2 * inner + c + step) % 8) for step in range(1, 8)]
    far_half = [(dp, 2 * (4 * outer + 2 * (1 - half) + k) + d) for k in range(2) for d in range(2)]

    barrier = pltpu.get_barrier_semaphore()
    greeted = [device for _, device in others] + [device for device in peers] + far_half
    for device in greeted:
        pl.semaphore_signal(barrier, inc=1, device_id=device, device_id_type=MESH)

    values = tokens[...].astype(f32)
    centre = values - jnp.mean(values, axis=1, keepdims=True)
    scale_inv = lax.rsqrt(jnp.mean(centre * centre, axis=1, keepdims=True) + epsilon)
    normed[...] = centre * scale_inv
    square = (TOKENS, TOKENS)
    lane, line = iota(square, 1), iota(square, 0)
    first, second = routes[:, 0:1], routes[:, 1:2]
    signed = (first == lane).astype(f32) - (second == lane).astype(f32)
    hit_first = (first == (lane >> 2)).astype(f32) * (lane < 16).astype(f32)
    hit_second = (second == (lane >> 2)).astype(f32) * (lane < 16).astype(f32)
    earlier = product(one_hot(line > lane), (hit_first + hit_second).astype(bf16), 1, 0)
    fits = (earlier == (lane & 3).astype(f32)).astype(f32)
    place_first, place_second = (hit_first * fits).astype(bf16), (hit_second * fits).astype(bf16)
    place_all = place_first + place_second
    arrange = (256, 256)
    to_message = one_hot(message_row(iota(arrange, 1)) == iota(arrange, 0))
    from_message = one_hot(message_row(iota(arrange, 0)) == iota(arrange, 1))
    pack = [one_hot(packed_row(iota((2 * ROWS, 256), 1), part_) == iota((2 * ROWS, 256), 0)) for part_ in range(2)]
    unpack = [one_hot(packed_row(iota((256, 2 * ROWS), 0), part_) == iota((256, 2 * ROWS), 1)) for part_ in range(2)]

    def messages(kind, chosen):
        low, high = chosen[:16, :HIDDEN // 2], chosen[:16, HIDDEN // 2:]
        sides = (jnp.where(half == 1, high, low), jnp.where(half == 1, low, high))
        stacked = jnp.concatenate(
            [side[:, LANES * i:LANES * (i + 1)] for side in sides for i in range(8)], axis=0
        ).astype(bf16)
        sends[kind] = product(to_message, stacked, 1, 0).astype(bf16).reshape(GROUP, 16, LANES)

    def returned(kind):
        stacked = product(from_message, hrecv[kind].reshape(256, LANES), 1, 0).astype(bf16).astype(f32)
        sides = [
            jnp.concatenate([stacked[16 * (8 * blk + i):16 * (8 * blk + i + 1)] for i in range(8)], axis=1)
            for blk in range(2)
        ]
        low, high = jnp.where(half == 1, sides[1], sides[0]), jnp.where(half == 1, sides[0], sides[1])
        rows = jnp.concatenate([low, high], axis=1)
        return jnp.concatenate([rows, jnp.zeros((TOKENS - 16, HIDDEN), f32)], axis=0).astype(bf16)

    messages(0, product(place_all, normed[...].astype(bf16), 0, 0))
    both = (16, LANES)
    edge = jnp.where(iota(both, 0) == 0, gain[...].astype(f32), jnp.where(iota(both, 0) == 1, bias[...].astype(f32), 0.0))
    for side in range(2):
        block[side, 0:64] = router[64 * side:64 * (side + 1)]
        block[side, 64:80] = edge.astype(bf16)
    held[c, dp] = block[c]
    recvs[0, me] = sends[0, me]

    pl.semaphore_wait(barrier, len(greeted))
    copies = Copies(send_sems, recv_sems)
    sent_n = [copies.start(sends.at[0, g], recvs.at[0, me], device) for g, device in others]
    sent_p = [copies.start(block.at[c], held.at[c, dp], peer) for peer in peers]
    got_w1 = copies.start(w1, wx1, over)
    got_w2 = copies.start(w2, wx2, over)

    def wait_for(found):
        for copy in found:
            copy.wait_recv()

    def place_rows(kind, feature_rows):
        for blk in range(2):
            ag[kind, blk, x, y] = feature_rows[blk].astype(bf16)

    def packed_rows(kind):
        rows = recvs[kind].reshape(256, LANES)
        both_halves = jnp.concatenate([product(pack[0], rows, 1, 0), product(pack[1], rows, 1, 0)], axis=1)
        return [both_halves[:ROWS], both_halves[ROWS:]]

    def gather_first(kind):
        return [copies.start(ag.at[kind, 0, x, y], ag.at[kind, 0, x, y], device) for device in along_y] + [
            copies.start(ag.at[kind, 1, x, y], ag.at[kind, 1, x, y], device) for device in along_x
        ]

    x_left, x_right, y_down, y_up = (x + 3) % SIDE, (x + 1) % SIDE, (y + 3) % SIDE, (y + 1) % SIDE
    pairs = (pl.ds(0, 2), pl.ds(2, 2))

    def gather_second(kind):
        def at(blk, place_, which):
            return ag.at[kind, 0, place_, pairs[which]] if blk == 0 else ag.at[kind, 1, pairs[which], place_]

        own, before, after = (x, y), (x_left, y_down), (x_right, y_up)
        ahead, back = (along_x[0], along_y[0]), (along_x[2], along_y[2])

        def move(blk, place_, which, device):
            return copies.start(at(blk, place_, which), at(blk, place_, which), device)

        one = [move(blk, own[blk], 0, ahead[blk]) for blk in range(2)]
        two = [move(blk, own[blk], 1, back[blk]) for blk in range(2)]
        rest = [move(blk, own[blk], 1, ahead[blk]) for blk in range(2)]
        rest += [move(blk, own[blk], 0, back[blk]) for blk in range(2)]
        for blk in range(2):
            one[blk].wait_recv()
            rest.append(move(blk, before[blk], 0, ahead[blk]))
        for blk in range(2):
            two[blk].wait_recv()
            rest.append(move(blk, after[blk], 1, back[blk]))
        return rest

    wait_for(sent_p)
    swap_router = copies.start(held.at[c], held.at[c], core)
    wait_for(sent_n)
    scaled_rows = []
    for blk, rows in enumerate(packed_rows(0)):
        spot = 2 * (4 * (half if blk == 0 else 1 - half) + near * 2 + c)
        parts = [held[c, spot + i, 64:80].astype(f32) for i in range(2)]
        gains = jnp.concatenate([parts[0][0:1], parts[1][0:1]], axis=1)
        biases = jnp.concatenate([parts[0][1:2], parts[1][1:2]], axis=1)
        scaled_rows.append(rows * gains + biases)
    place_rows(0, scaled_rows)
    begun_n = gather_first(0)

    swap_router.wait_recv()
    for block_id in range(GROUP):
        for side in range(2):
            rt[128 * block_id + 64 * side:128 * block_id + 64 * (side + 1)] = held[side, block_id, 0:64]
    gain_all = jnp.concatenate([held[0, i, 64:80].astype(f32)[0:1] for i in range(GROUP)], axis=1)
    bias_all = jnp.concatenate([held[0, i, 64:80].astype(f32)[1:2] for i in range(GROUP)], axis=1)
    normal = (normed[...] * gain_all + bias_all).astype(bf16)
    logits = product(normal, rt[...], 1, 0)
    gap = jnp.sum(logits * signed, axis=1, keepdims=True)
    gate_first, gate_second = jax.nn.sigmoid(gap), jax.nn.sigmoid(-gap)
    cot_f = cot[...].astype(f32)
    messages(
        1,
        product(place_first, (gate_first * cot_f).astype(bf16), 0, 0)
        + product(place_second, (gate_second * cot_f).astype(bf16), 0, 0),
    )
    recvs[1, me] = sends[1, me]
    sent_s = [copies.start(sends.at[1, g], recvs.at[1, me], device) for g, device in others]
    wait_for(begun_n)
    rest_n = gather_second(0)
    wait_for(rest_n)

    def rows_of(kind, blk, group):
        return ag[kind, blk, group].reshape(CHUNK, WIDTH)

    def partial_sum(kind, group):
        if kind == 0:
            return product(rows_of(0, 0, group), w1[...], 1, 0) + product(rows_of(0, 1, group), wx1[...], 1, 0)
        return product(rows_of(1, 0, group), w2[...], 1, 1) + product(rows_of(1, 1, group), wx2[...], 1, 1)

    mine = [(x + c) % SIDE, (x + 3 - c) % SIDE]
    theirs = [(x + 1 - c) % SIDE, (x + 2 + c) % SIDE]
    zoned = {}

    def begin(kind):
        crossed = []
        for j in range(2):
            cs[kind, j] = partial_sum(kind, theirs[j]).astype(bf16)
            crossed.append(copies.start(cs.at[kind, j], cr.at[kind, j], core))
        for j in range(2):
            pown[kind, j] = partial_sum(kind, mine[j])
        for j in range(2):
            crossed[j].wait_recv()
            zs[kind, j] = (pown[kind, j] + cr[kind, j].astype(f32)).astype(bf16)
            zoned[kind, j] = copies.start(zs.at[kind, j], zr.at[kind, j], beside)

    def whole(kind, j):
        zoned[kind, j].wait_recv()
        return zs[kind, j].astype(f32) + zr[kind, j].astype(f32)

    def spread(kind, values_of, weight_a, weight_b, right_dim):
        for group in range(SIDE):
            chunk = values_of[group]
            for blk, weight in ((0, weight_a), (1, weight_b)):
                part[kind, blk, group] = product(chunk, weight[...], 1, right_dim).astype(bf16).reshape(SIDE, ROWS, WIDTH)

    def reduce_first(kind):
        found = []
        for step in range(1, SIDE):
            found.append(copies.start(part.at[kind, 0, (x + step) % SIDE], rs1.at[kind, 0, step - 1], along_x[step - 1]))
            found.append(copies.start(part.at[kind, 1, :, (y + step) % SIDE], rs1.at[kind, 1, step - 1], along_y[step - 1]))
        return found

    def reduce_second(kind, found):
        wait_for(found)
        for blk in range(2):
            own = part[kind, 0, x] if blk == 0 else part[kind, 1, :, y]
            total = own.astype(f32)
            for step in range(SIDE - 1):
                total = total + rs1[kind, blk, step].astype(f32)
            mid[kind, blk] = total.astype(bf16)
        again = []
        for step in range(1, SIDE):
            again.append(copies.start(mid.at[kind, 0, (y + step) % SIDE], rs2.at[kind, 0, step - 1], along_y[step - 1]))
            again.append(copies.start(mid.at[kind, 1, (x + step) % SIDE], rs2.at[kind, 1, step - 1], along_x[step - 1]))
        return again

    def send_home(kind, again):
        wait_for(again)
        ends = []
        for blk in range(2):
            total = mid[kind, blk, y if blk == 0 else x].astype(f32)
            for step in range(SIDE - 1):
                total = total + rs2[kind, blk, step].astype(f32)
            ends.append(total.astype(bf16))
        rows = jnp.concatenate(ends, axis=0)
        out = product(unpack[0], rows[:, :LANES], 1, 0) + product(unpack[1], rows[:, LANES:], 1, 0)
        hsend[kind] = out.astype(bf16).reshape(GROUP, 16, LANES)
        hrecv[kind, me] = hsend[kind, me]
        return [copies.start(hsend.at[kind, g], hrecv.at[kind, me], device) for g, device in others]

    got_w1.wait_recv()
    begin(0)
    wait_for(sent_s)
    place_rows(1, packed_rows(1))
    wait_for(gather_first(1))
    wait_for(gather_second(1))
    got_w2.wait_recv()
    begin(1)
    shared = []
    for j in range(2):
        value, grade = gelu_parts(whole(0, j))
        act[mine[j]] = value.astype(bf16)
        shared.append(copies.start(act.at[mine[j]], act.at[mine[j]], core))
        slope[j] = grade
    wait_for(shared)
    spread(0, act, w2, wx2, 0)
    found_out = reduce_first(0)
    active = act[...].reshape(SIDE * CHUNK, UNITS)
    gds[...] = product(active, ag[1, 1].reshape(SIDE * CHUNK, WIDTH), 0, 0).astype(bf16)
    got_gd = copies.start(gds, gdr, over)
    gd_own[...] = product(active, ag[1, 0].reshape(SIDE * CHUNK, WIDTH), 0, 0)
    again_out = reduce_second(0, found_out)
    shared = []
    for j in range(2):
        gh[mine[j]] = (whole(1, j) * slope[j]).astype(bf16)
        shared.append(copies.start(gh.at[mine[j]], gh.at[mine[j]], core))
    home_out = send_home(0, again_out)
    wait_for(shared)
    spread(1, gh, w1, wx1, 1)
    found_in = reduce_first(1)
    grads = gh[...].reshape(SIDE * CHUNK, UNITS)
    gus[...] = product(ag[0, 1].reshape(SIDE * CHUNK, WIDTH), grads, 0, 0).astype(bf16)
    got_gu = copies.start(gus, gur, over)
    gu_own[...] = product(ag[0, 0].reshape(SIDE * CHUNK, WIDTH), grads, 0, 0)

    wait_for(home_out)
    rows = returned(0)
    out_first, out_second = product(place_first, rows, 1, 0), product(place_second, rows, 1, 0)
    moe_out[...] = (gate_first * out_first + gate_second * out_second).astype(bf16)
    gap_grad = jnp.sum(cot[...].astype(f32) * (out_first - out_second), axis=1, keepdims=True) * gate_first * gate_second
    base[...] = gap_grad * product(signed.astype(bf16), rt[...], 1, 1)
    normal = (normed[...] * gain_all + bias_all).astype(bf16)
    local = product(normal, (gap_grad * signed).astype(bf16), 0, 0).astype(bf16)
    for block_id in range(GROUP):
        for side in range(2):
            for path in range(2):
                begin_row = 128 * block_id + 64 * side + 32 * path
                lr[side, path, block_id // SIDE, block_id % SIDE] = local[begin_row:begin_row + 32]

    cored = copies.start(lr.at[1 - c], lc, core)
    again_in = reduce_second(1, found_in)
    cored.wait_recv()
    l0[...] = (lr[c].astype(f32) + lc[...].astype(f32)).astype(bf16)
    sent = []
    for step in range(1, SIDE):
        sent.append(copies.start(l0.at[0, (x + step) % SIDE], l1.at[0, step - 1], along_x[step - 1]))
        sent.append(copies.start(l0.at[1, :, (y + step) % SIDE], l1.at[1, step - 1], along_y[step - 1]))
    home_in = send_home(1, again_in)
    wait_for(sent)
    for path in range(2):
        own = l0[0, x] if path == 0 else l0[1, :, y]
        l2[path] = (own.astype(f32) + l1[path, 0].astype(f32) + l1[path, 1].astype(f32) + l1[path, 2].astype(f32)).astype(bf16)
    sent = []
    for step in range(1, SIDE):
        sent.append(copies.start(l2.at[0, (y + step) % SIDE], l3.at[0, step - 1], along_y[step - 1]))
        sent.append(copies.start(l2.at[1, (x + step) % SIDE], l3.at[1, step - 1], along_x[step - 1]))
    wait_for(sent)
    for path in range(2):
        own = l2[path, y if path == 0 else x]
        total = (own.astype(f32) + l3[path, 0].astype(f32)) + (l3[path, 1].astype(f32) + l3[path, 2].astype(f32))
        l4[2 * path] = total[0:16].astype(bf16)
        l4[2 * path + 1] = total[16:32].astype(bf16)
    sent_l = [copies.start(l4.at[(inner + step) % 4], l5.at[step - 1], along_in[step - 1]) for step in range(1, 4)]

    wait_for(home_in)
    grad_normal = product(place_all, returned(1), 1, 0) + base[...]
    gains = jnp.sum(grad_normal * normed[...], axis=0, keepdims=True)
    biases = jnp.sum(grad_normal, axis=0, keepdims=True)
    wide = (8, HIDDEN)
    dense = jnp.where(iota(wide, 0) == 0, gains, jnp.where(iota(wide, 0) == 1, biases, 0.0))
    for block_id in range(GROUP):
        gb[block_id] = dense[:, 128 * block_id:128 * (block_id + 1)]
    sent_g = [
        copies.start(gb.at[(dp + step) % GROUP], gbr.at[step - 1], peer) for step, peer in enumerate(peers, 1)
    ]
    wait_for(sent_l)
    l6[...] = (
        (l4[inner].astype(f32) + l5[0].astype(f32)) + (l5[1].astype(f32) + l5[2].astype(f32))
    ).astype(bf16)
    sent_l = [copies.start(l6, l7.at[outer], device) for device in along_out]
    l7[outer] = l6[...]
    grad_norm = grad_normal * gain_all
    mean_grad = jnp.mean(grad_norm, axis=1, keepdims=True)
    mean_both = jnp.mean(grad_norm * normed[...], axis=1, keepdims=True)
    grad_in[...] = (scale_inv * (grad_norm - mean_grad - normed[...] * mean_both)).astype(bf16)
    wait_for(sent_g)
    total = gb[dp]
    for step in range(GROUP - 1):
        total = total + gbr[step]
    gb1[...] = total
    gb2[2 * inner + c] = total
    sent_g = [copies.start(gb1, gb2.at[2 * inner + c], device) for device in octet]
    wait_for(sent_l)
    l8[inner] = ((l7[0].astype(f32) + l7[1].astype(f32)) + (l7[2].astype(f32) + l7[3].astype(f32))).astype(bf16)
    sent_l = [copies.start(l8.at[inner], l8.at[inner], device) for device in along_in]
    wait_for(sent_g)
    total = gb2[0]
    for i in range(1, 8):
        total = total + gb2[i]
    gb3[outer] = total
    sent_g = [copies.start(gb3.at[outer], gb3.at[outer], device) for device in along_out]
    got_gd.wait_recv()
    gd_out[...] = (gd_own[...] + gdr[...].astype(f32)).astype(bf16)
    wait_for(sent_l)
    fin[c] = l8[...]
    last = copies.start(fin.at[c], fin.at[c], core)
    got_gu.wait_recv()
    gu_out[...] = (gu_own[...] + gur[...].astype(f32)).astype(bf16)
    wait_for(sent_g)
    dense_out[...] = (gb3[0] + gb3[1]) + (gb3[2] + gb3[3])
    last.wait_recv()
    router_out[...] = fin[...].astype(f32).reshape(128, 128)
    copies.finish()


def on_device(tokens, cotangent, routes, ln_gain, ln_bias, router_weight, up_weight, down_weight):
    vmem = pl.BlockSpec(memory_space=pltpu.VMEM)
    pair = (2, 2, CHUNK, UNITS)
    moved = (2, 2, SIDE, SIDE, ROWS, WIDTH)
    dense = (8, LANES)
    scratch = [
        ((TOKENS, HIDDEN), f32),
        ((2, 80, LANES), bf16),
        ((2, GROUP, 80, LANES), bf16),
        ((HIDDEN, LANES), bf16),
        ((2, GROUP, 16, LANES), bf16),
        ((2, GROUP, 16, LANES), bf16),
        (moved, bf16),
        ((WIDTH, UNITS), bf16),
        ((UNITS, WIDTH), bf16),
        (pair, f32),
        (pair, bf16),
        (pair, bf16),
        (pair, bf16),
        (pair, bf16),
        ((SIDE, CHUNK, UNITS), bf16),
        ((SIDE, CHUNK, UNITS), bf16),
        ((2, CHUNK, UNITS), f32),
        (moved, bf16),
        ((2, 2, SIDE - 1, SIDE, ROWS, WIDTH), bf16),
        ((2, 2, SIDE, ROWS, WIDTH), bf16),
        ((2, 2, SIDE - 1, ROWS, WIDTH), bf16),
        ((2, GROUP, 16, LANES), bf16),
        ((2, GROUP, 16, LANES), bf16),
        ((UNITS, WIDTH), bf16),
        ((UNITS, WIDTH), bf16),
        ((WIDTH, UNITS), bf16),
        ((WIDTH, UNITS), bf16),
        ((UNITS, WIDTH), f32),
        ((WIDTH, UNITS), f32),
        ((TOKENS, HIDDEN), f32),
        ((2, 2, SIDE, SIDE, 32, LANES), bf16),
        ((2, SIDE, SIDE, 32, LANES), bf16),
        ((2, SIDE, SIDE, 32, LANES), bf16),
        ((2, SIDE - 1, SIDE, 32, LANES), bf16),
        ((2, SIDE, 32, LANES), bf16),
        ((2, SIDE - 1, 32, LANES), bf16),
        ((4, 16, LANES), bf16),
        ((3, 16, LANES), bf16),
        ((16, LANES), bf16),
        ((4, 16, LANES), bf16),
        ((4, 16, LANES), bf16),
        ((2, 4, 16, LANES), bf16),
        ((GROUP,) + dense, f32),
        ((GROUP - 1,) + dense, f32),
        (dense, f32),
        ((8,) + dense, f32),
        ((4,) + dense, f32),
    ]
    count = 224
    moe_out, grad_input, grad_up, grad_down, grad_router, grad_dense = pl.pallas_call(
        step_kernel,
        out_shape=[
            jax.ShapeDtypeStruct(tokens.shape, bf16),
            jax.ShapeDtypeStruct(tokens.shape, bf16),
            jax.ShapeDtypeStruct((WIDTH, UNITS), bf16),
            jax.ShapeDtypeStruct((UNITS, WIDTH), bf16),
            jax.ShapeDtypeStruct((128, LANES), f32),
            jax.ShapeDtypeStruct(dense, f32),
        ],
        in_specs=[vmem] * 8,
        out_specs=[vmem] * 6,
        scratch_shapes=[pltpu.VMEM(shape, kind) for shape, kind in scratch]
        + [pltpu.SemaphoreType.DMA((count,)), pltpu.SemaphoreType.DMA((count,))],
        compiler_params=pltpu.CompilerParams(collective_id=0, has_side_effects=True, vmem_limit_bytes=56 << 20),
    )(tokens, cotangent, routes, ln_gain[None], ln_bias[None], router_weight, up_weight[0], down_weight[0])
    return (moe_out, grad_input, grad_up[None], grad_down[None], grad_router, grad_dense[0], grad_dense[1])


def solution(mesh):
    return jax.shard_map(
        on_device,
        mesh=mesh,
        in_specs=(
            P(("dp", "expert"), None),
            P(("dp", "expert"), None),
            P(("dp", "expert"), None),
            P("dp"),
            P("dp"),
            P("dp", None),
            P("expert", None, "dp"),
            P("expert", "dp", None),
        ),
        out_specs=(
            P(("dp", "expert"), None),
            P(("dp", "expert"), None),
            P("expert", None, "dp"),
            P("expert", "dp", None),
            P("dp", None),
            P("dp"),
            P("dp"),
        ),
        check_vma=False,
    )
```

time: 805 us -> 135 us (0.17)
  waiting for transfers between devices: 401 us -> 0 us
  blocking collectives: 275 us -> 0 us
  Pallas kernels: 0 us -> 126 us
  starting transfers between devices: 55.6 us -> 0 us
  matrix products: 18.3 us -> 0 us
  other arithmetic: 17.7 us -> 0 us
  between operations: 14.9 us -> 0.65 us
  local copies, waits for them, and re-layouts: 19.7 us -> 8.26 us
    ppermute x6 -> x0, waiting for transfers between devices: 217 us -> none  [partner_2(): return lax.ppermute(block, axis, route)]
    unnamed x5 -> x0, waiting for transfers between devices: 143 us -> none
    pallas_call x0 -> x1, Pallas kernels: none -> 126 us  [on_device(): pl.pallas_call(step_kernel, out_shape=[jax.ShapeDtypeStruct(tokens.shape,...]
    psum x1 -> x0, blocking collectives: 90.6 us -> none  [on_device(): lax.psum(part_router.astype(jnp.bfloat16), 'expert').astype(jnp.float32)]
    all_gather x5 -> x0, blocking collectives: 86.4 us -> none  [the longest x1 19.5 us: on_device(): lax.all_gather(router_weight, 'dp', axis=0, tiled=True)]
    all_to_all x2 -> x0, blocking collectives: 66.7 us -> none  [the longest x1 37.9 us: on_device(): lax.all_to_all(send_normal, 'expert', split_axis=0, concat_axis=0, tiled=...]
    unnamed x1 -> x0, blocking collectives: 31.5 us -> none
    all_to_all x2 -> x0, starting transfers between devices: 29.2 us -> none  [the longest x1 14.6 us: send_home(): lax.all_to_all(out_sum[0].astype(jnp.bfloat16), 'expert', split_axis=0, c...]
  transfers between devices with their start and end apart: 11 -> 0, of which waited for: 10 -> 0; matrix products, arithmetic and copies ran while one was open for 2% -> 0% of each run, Pallas kernels for 0% -> 0%
where the time goes in v2:
time: 135 us
  Pallas kernels  126 us (93%)
  local copies, waits for them, and re-layouts  8.26 us (6%)
    pallas_call x1, Pallas kernels, on_device(): pl.pallas_call(step_kernel, out_shape=[jax.ShapeDtypeStruct(tokens.shape,...  126 us
    unnamed x14, local copies, waits for them, and re-layouts  6.98 us

profile of v2, /device:TPU:1, one launch (start us, length us, event | category | flops | bytes accessed | tf_op | source)
XLA Modules:
  0.0 134.6 jit_solution(17071635083228652747)
XLA Ops:
  0.6 1.4 %copy.15.routes = s32[128,2]{1,0:T(8,128)} copy(s32[128,2]{0,1:T(2,128)} %param.10) | data formatting | bytes 2048 | tf_op args[2]
  2.0 125.7 %shard_map.135 = (bf16[128,2048]{1,0:T(8,128)(2,1)}, bf16[128,2048]{1,0:T(8,128)(2,1)}, bf16[256,512]{1,0:T(8,128)(2,1)}, bf16[512,256]{1,0:T(8,128)(2,1)}, f32[128,128]{1,0:T(8,128)}, /*index=5*/f32[8,128]{1,0:T(8,128)}) custom-call(bf16[128,2048]{1,0:T(8,128)(2,1)} %tokens.1, bf16[128,2048]{1,0:T(8,128)(2,1)} %cot.1, s32[128,2]{1,0:T(8,128)} %copy.15.routes, ...), custom_call_target="tpu_custom_call" | custom-call | tf_op jit(solution)/shard_map/pallas_call | solution.py:511
  127.8 1.3 slice_bitcast_fusion
  129.1 0.0 copy-start
  129.1 1.9 %copy.21 = bf16[128,2048]{1,0:T(8,128)(2,1)} copy(bf16[128,2048]{1,0:T(8,128)(2,1)} %get-tuple-element.28) | data formatting | bytes 1048576
  131.0 0.0 copy-done
  131.0 0.0 copy-start.2
  131.0 0.8 copy.22
  131.8 0.3 copy-done.2
  132.1 0.0 copy-start.1
  132.1 0.7 copy.23
  132.8 0.3 copy-done.1
  133.1 0.0 copy-start.3
  133.1 0.7 copy.24
  133.8 0.2 copy-done.3
  134.0 0.6 copy.25
Async XLA Ops:
  129.1 1.9 %copy-start = (bf16[128,2048]{1,0:T(8,128)(2,1)S(1)}, bf16[128,2048]{1,0:T(8,128)(2,1)}, u32[]{:S(2)}) copy-start(bf16[128,2048]{1,0:T(8,128)(2,1)} %get-tuple-element.29) | copy-start | bytes 1572868
  131.0 1.1 copy-start.2
  132.1 1.0 copy-start.1
  133.1 0.9 copy-start.3

commit v3 on v2

v3 whole, which is shorter than its diff:
```python
import jax
import jax.numpy as jnp
from jax import lax
from jax.experimental import pallas as pl
from jax.experimental.pallas import tpu as pltpu
from jax.sharding import PartitionSpec as P

SLICES = 8
CAP = 3
SLOTS = 4
SIDE = 4
GROUP = 16
WIDTH = 256
LANES = 128
HIDDEN = 2048
TOKENS = 128
UNITS = 512
ROWS = 48
CHUNK = SIDE * ROWS
MESH = pl.DeviceIdType.MESH

epsilon = 1e-05
root_half = 0.7071067811865476
inv_root_tau = 0.3989422804014327
f32 = jnp.float32
bf16 = jnp.bfloat16


def gelu_parts(hidden):
    normal_cdf = 0.5 * (1.0 + lax.erf(hidden * root_half))
    density = inv_root_tau * jnp.exp(-0.5 * hidden * hidden)
    return (hidden * normal_cdf, normal_cdf + hidden * density)


class Copies:
    def __init__(self, send_sems, recv_sems):
        self.send_sems, self.recv_sems, self.made = send_sems, recv_sems, []

    def start(self, src, dst, device):
        index = len(self.made)
        copy = pltpu.make_async_remote_copy(
            src_ref=src,
            dst_ref=dst,
            send_sem=self.send_sems.at[index],
            recv_sem=self.recv_sems.at[index],
            device_id=device,
            device_id_type=MESH,
        )
        copy.start()
        self.made.append(copy)
        return copy

    def finish(self):
        for copy in self.made:
            copy.wait_send()


def place():
    dp = lax.axis_index("dp")
    ex = lax.axis_index("expert")
    return dp // SIDE, dp % SIDE, ex // 2, ex % 2, dp, ex


def x_partner(step, x, y, ex):
    return (((x + step) % SIDE) * SIDE + y, ex)


def y_partner(step, x, y, ex):
    return (x * SIDE + (y + step) % SIDE, ex)


def product(left, right, left_dim, right_dim):
    return lax.dot_general(left, right, (((left_dim,), (right_dim,)), ((), ())), preferred_element_type=f32)


def iota(shape, dim):
    return lax.broadcasted_iota(jnp.int32, shape, dim)


def one_hot(found):
    return found.astype(f32).astype(bf16)


def message_row(row):
    slot, expert = row & 3, (row >> 2) & 3
    lane_half, k2, blk = (row >> 4) & 1, (row >> 5) & 3, row >> 7
    return (expert * 4 + k2) * 16 + blk * 8 + lane_half * 4 + slot


def packed_row(row, lane_half):
    slot = row & 3
    good = (slot < CAP) & (((row >> 2) & 1) == lane_half)
    return jnp.where(good, ((row >> 3) & 1) * ROWS + (row >> 4) * CAP + slot, -1)


def step_kernel(
    tokens, cot, routes, gain, bias, router, w1, w2,
    moe_out, grad_in, gu_out, gd_out, router_out, gain_out, bias_out,
    normed, block, held, rt, sends, recvs, ag, wx1, wx2, pown, cs, cr, zs, zr, act, gh, slope, part, rs1, mid, rs2,
    hsend, hrecv, gds, gdr, gus, gur, gd_own, gu_own, base,
    lr, lc, l0, l1, l2, l3, l4, l5, l6, l7, fin, nrm, gb, gbr, gb1, gb2, gb3,
    parts_out, parts_in, dot_send, dot_home,
    send_sems, recv_sems,
):
    x, y, z, c, dp, ex = place()
    outer, inner = z // 4, z % 4
    half, near = inner % 2, inner // 2
    me = outer * 4 + near * 2 + c

    def member(step):
        g = (me + step) % GROUP
        return g, (dp, 2 * (4 * (g // 4) + 2 * ((g % 4) // 2) + half) + g % 2)

    others = [member(step) for step in range(1, GROUP)]
    peers = [((dp + step) % GROUP, ex) for step in range(1, GROUP)]
    along_x = [x_partner(step, x, y, ex) for step in range(1, SIDE)]
    along_y = [y_partner(step, x, y, ex) for step in range(1, SIDE)]
    core = (dp, 2 * z + 1 - c)
    beside = (dp, 2 * (z + 2 - 4 * near) + c)
    over = (dp, 2 * (z + 1 - 2 * half) + c)
    along_in = [(dp, 2 * (outer * 4 + (inner + step) % 4) + c) for step in range(1, 4)]
    along_out = [(dp, 2 * ((outer + step) % 4 * 4 + inner) + c) for step in range(1, 4)]
    octet = [(dp, 8 * outer + (2 * inner + c + step) % 8) for step in range(1, 8)]
    far_half = [(dp, 2 * (4 * outer + 2 * k + 1 - half) + d) for k in range(2) for d in range(2)]

    barrier = pltpu.get_barrier_semaphore()
    greeted = [device for _, device in others] + [device for device in peers] + far_half
    for device in greeted:
        pl.semaphore_signal(barrier, inc=1, device_id=device, device_id_type=MESH)

    def norm(rows):
        values = rows.astype(f32)
        centre = values - jnp.mean(values, axis=1, keepdims=True)
        scale = lax.rsqrt(jnp.mean(centre * centre, axis=1, keepdims=True) + epsilon)
        return centre * scale, scale

    square = (TOKENS, TOKENS)
    lane, line = iota(square, 1), iota(square, 0)
    diagonal = (lane == line).astype(f32)
    named = routes[...].astype(f32)
    first, second = (
        jnp.sum(diagonal * named[k:k + 1], axis=1, keepdims=True).astype(jnp.int32) for k in range(2)
    )
    signed = (first == lane).astype(f32) - (second == lane).astype(f32)
    hit_first = (first == (lane >> 2)).astype(f32) * (lane < 16).astype(f32)
    hit_second = (second == (lane >> 2)).astype(f32) * (lane < 16).astype(f32)
    earlier = product(one_hot(line > lane), (hit_first + hit_second).astype(bf16), 1, 0)
    fits = (earlier == (lane & 3).astype(f32)).astype(f32)
    place_first, place_second = (hit_first * fits).astype(bf16), (hit_second * fits).astype(bf16)
    place_all = place_first + place_second
    arrange = (256, 256)
    to_message = one_hot(message_row(iota(arrange, 1)) == iota(arrange, 0))

    def messages(kind, chosen):
        low, high = (
            jnp.concatenate(
                [chosen[:16, LANES * i:LANES * (i + 1)] for k in (0, 8) for i in range(k + 4 * side, k + 4 * side + 4)],
                axis=0,
            )
            for side in range(2)
        )
        stacked = jnp.concatenate(
            [jnp.where(half == 1, high, low), jnp.where(half == 1, low, high)], axis=0
        ).astype(bf16)
        sends[kind] = product(to_message, stacked, 1, 0).astype(bf16).reshape(GROUP, 16, LANES)

    def returned(kind):
        stacked = product(from_message, hrecv[kind].reshape(256, LANES), 1, 0).astype(bf16).astype(f32)
        sides = [stacked[:TOKENS], stacked[TOKENS:]]
        sides = [jnp.where(half == 1, sides[1], sides[0]), jnp.where(half == 1, sides[0], sides[1])]
        rows = jnp.concatenate(
            [sides[side][16 * i:16 * (i + 1)] for k in (0, 4) for side in range(2) for i in range(k, k + 4)], axis=1
        )
        return jnp.concatenate([rows, jnp.zeros((TOKENS - 16, HIDDEN), f32)], axis=0).astype(bf16)

    messages(0, norm(product(place_all, tokens[...], 0, 0)[:16])[0])
    both = (16, LANES)
    edge = jnp.where(iota(both, 0) == 0, gain[...].astype(f32), jnp.where(iota(both, 0) == 1, bias[...].astype(f32), 0.0))
    for side in range(2):
        block[side, 0:64] = router[64 * side:64 * (side + 1)]
        block[side, 64:80] = edge.astype(bf16)
    held[c, dp] = block[c]
    recvs[0, me] = sends[0, me]

    pl.semaphore_wait(barrier, len(greeted))
    copies = Copies(send_sems, recv_sems)
    sent_n = [copies.start(sends.at[0, g], recvs.at[0, me], device) for g, device in others]
    sent_p = [copies.start(block.at[c], held.at[c, dp], peer) for peer in peers]
    got_w1 = copies.start(w1, wx1, over)
    from_message = one_hot(message_row(iota(arrange, 0)) == iota(arrange, 1))
    normed_value, scale_inv = norm(tokens[...])
    normed[...] = normed_value
    parts_out[...] = jnp.zeros_like(parts_out)
    pack = [one_hot(packed_row(iota((2 * ROWS, 256), 1), part_) == iota((2 * ROWS, 256), 0)) for part_ in range(2)]
    unpack = [one_hot(packed_row(iota((256, 2 * ROWS), 0), part_) == iota((256, 2 * ROWS), 1)) for part_ in range(2)]

    def wait_for(found):
        for copy in found:
            copy.wait_recv()

    def place_rows(kind, feature_rows):
        for blk in range(2):
            ag[kind, blk, x, y] = feature_rows[blk].astype(bf16)

    def packed_rows(kind):
        rows = recvs[kind].reshape(256, LANES)
        both_halves = jnp.concatenate([product(pack[0], rows, 1, 0), product(pack[1], rows, 1, 0)], axis=1)
        return [both_halves[:ROWS], both_halves[ROWS:]]

    def gather_first(kind):
        return [copies.start(ag.at[kind, 0, x, y], ag.at[kind, 0, x, y], device) for device in along_y] + [
            copies.start(ag.at[kind, 1, x, y], ag.at[kind, 1, x, y], device) for device in along_x
        ]

    x_left, x_right, y_down, y_up = (x + 3) % SIDE, (x + 1) % SIDE, (y + 3) % SIDE, (y + 1) % SIDE
    pairs = (pl.ds(0, 2), pl.ds(2, 2))

    def at(kind, blk, place_, which):
        return ag.at[kind, 0, place_, pairs[which]] if blk == 0 else ag.at[kind, 1, pairs[which], place_]

    own, before, after = (x, y), (x_left, y_down), (x_right, y_up)
    ahead, back = (along_x[0], along_y[0]), (along_x[2], along_y[2])

    def move(kind, blk, place_, which, device):
        return copies.start(at(kind, blk, place_[blk], which), at(kind, blk, place_[blk], which), device[blk])

    def gather_second(kind):
        one = [move(kind, blk, own, 0, ahead) for blk in range(2)]
        two = [move(kind, blk, own, 1, back) for blk in range(2)]
        rest = [move(kind, blk, own, 1, ahead) for blk in range(2)]
        return one, two, rest + [move(kind, blk, own, 0, back) for blk in range(2)]

    def gather_last(kind, begun):
        one, two, rest = begun
        rest = list(rest)
        for blk in range(2):
            one[blk].wait_recv()
            rest.append(move(kind, blk, before, 0, ahead))
        for blk in range(2):
            two[blk].wait_recv()
            rest.append(move(kind, blk, after, 1, back))
        return rest

    wait_for(sent_p)
    swap_router = copies.start(held.at[c], held.at[c], core)
    edges = [held[c, i, 64:80].astype(f32) for i in range(GROUP)]
    gain_all = jnp.concatenate([edge_rows[0:1] for edge_rows in edges], axis=1)
    bias_all = jnp.concatenate([edge_rows[1:2] for edge_rows in edges], axis=1)
    normal = (normed[...] * gain_all + bias_all).astype(bf16)
    swap_router.wait_recv()
    for block_id in range(GROUP):
        for side in range(2):
            rt[128 * block_id + 64 * side:128 * block_id + 64 * (side + 1)] = held[side, block_id, 0:64]
    logits = product(normal, rt[...], 1, 0)
    gap = jnp.sum(logits * signed, axis=1, keepdims=True)
    gate_first, gate_second = jax.nn.sigmoid(gap), jax.nn.sigmoid(-gap)
    cot_f = cot[...].astype(f32)
    messages(
        1,
        product(place_first, (gate_first * cot_f).astype(bf16), 0, 0)[:16]
        + product(place_second, (gate_second * cot_f).astype(bf16), 0, 0)[:16],
    )
    recvs[1, me] = sends[1, me]
    sent_s = [copies.start(sends.at[1, g], recvs.at[1, me], device) for g, device in others]
    got_w2 = copies.start(w2, wx2, over)

    wait_for(sent_n)
    place_rows(0, packed_rows(0))
    begun_n = gather_first(0)
    wait_for(begun_n)
    second_n = gather_second(0)
    wait_for(sent_s)
    place_rows(1, packed_rows(1))
    begun_s = gather_first(1)
    last_n = gather_last(0, second_n)
    wait_for(begun_s)
    second_s = gather_second(1)
    wait_for(last_n)
    spots = [2 * (4 * near + 2 * (half if blk == 0 else 1 - half) + c) for blk in range(2)]
    for blk in range(2):
        parts = [held[c, spots[blk] + i, 64:80].astype(f32) for i in range(2)]
        gains = jnp.concatenate([parts[0][0:1], parts[1][0:1]], axis=1)
        biases = jnp.concatenate([parts[0][1:2], parts[1][1:2]], axis=1)
        for group in range(SIDE):
            rows = ag[0, blk, group].reshape(CHUNK, WIDTH).astype(f32)
            nrm[blk, group] = (rows * gains + biases).astype(bf16)

    def rows_of(kind, blk, group):
        return nrm[blk, group] if kind == 0 else ag[1, blk, group].reshape(CHUNK, WIDTH)

    def partial_sum(kind, group):
        if kind == 0:
            return product(rows_of(0, 0, group), w1[...], 1, 0) + product(rows_of(0, 1, group), wx1[...], 1, 0)
        return product(rows_of(1, 0, group), w2[...], 1, 1) + product(rows_of(1, 1, group), wx2[...], 1, 1)

    mine = [(x + c) % SIDE, (x + 3 - c) % SIDE]
    theirs = [(x + 1 - c) % SIDE, (x + 2 + c) % SIDE]
    zoned = {}

    def begin(kind):
        crossed = []
        for j in range(2):
            cs[kind, j] = partial_sum(kind, theirs[j]).astype(bf16)
            crossed.append(copies.start(cs.at[kind, j], cr.at[kind, j], core))
        for j in range(2):
            pown[kind, j] = partial_sum(kind, mine[j])
        for j in range(2):
            crossed[j].wait_recv()
            zs[kind, j] = (pown[kind, j] + cr[kind, j].astype(f32)).astype(bf16)
            zoned[kind, j] = copies.start(zs.at[kind, j], zr.at[kind, j], beside)

    def whole(kind, j):
        zoned[kind, j].wait_recv()
        return zs[kind, j].astype(f32) + zr[kind, j].astype(f32)

    ones = jnp.ones((8, WIDTH), bf16)
    sums = ([], [])

    def summed(values):
        return jnp.sum(values, axis=0, keepdims=True)

    def two_rows(gains, biases):
        wide = (8, gains.shape[1])
        return jnp.where(iota(wide, 0) == 0, gains, jnp.where(iota(wide, 0) == 1, biases, 0.0))

    def spread(kind, values_of, weight_a, weight_b, right_dim, groups=tuple(range(SIDE))):
        for group in groups:
            chunk = values_of[group]
            dots = [None] * SIDE
            for blk, weight in ((0, weight_a), (1, weight_b)):
                term = product(chunk, weight[...], 1, right_dim)
                part[kind, blk, group] = term.astype(bf16).reshape(SIDE, ROWS, WIDTH)
                both_rows = term * ag[1 - kind, blk, group].reshape(CHUNK, WIDTH).astype(f32)
                if kind == 0:
                    low_rows = both_rows.astype(bf16)
                    for line_y in range(SIDE):
                        dot = product(ones, low_rows[ROWS * line_y:ROWS * (line_y + 1)], 1, 1)
                        dots[line_y] = dot if dots[line_y] is None else dots[line_y] + dot
                else:
                    gains, biases = summed(both_rows), summed(term)
                    sums[blk].append((gains, biases))
            if kind == 0:
                for line_y in range(SIDE):
                    parts_out[SIDE * group + line_y, :, 0:ROWS] = dots[line_y]

    def reduce_first(kind):
        found = []
        for step in range(1, SIDE):
            found.append(copies.start(part.at[kind, 0, (x + step) % SIDE], rs1.at[kind, 0, step - 1], along_x[step - 1]))
            found.append(copies.start(part.at[kind, 1, :, (y + step) % SIDE], rs1.at[kind, 1, step - 1], along_y[step - 1]))
        return found

    def reduce_second(kind, found):
        wait_for(found)
        for blk in range(2):
            own = part[kind, 0, x] if blk == 0 else part[kind, 1, :, y]
            total = own.astype(f32)
            for step in range(SIDE - 1):
                total = total + rs1[kind, blk, step].astype(f32)
            mid[kind, blk] = total.astype(bf16)
        again = []
        for step in range(1, SIDE):
            again.append(copies.start(mid.at[kind, 0, (y + step) % SIDE], rs2.at[kind, 0, step - 1], along_y[step - 1]))
            again.append(copies.start(mid.at[kind, 1, (x + step) % SIDE], rs2.at[kind, 1, step - 1], along_x[step - 1]))
        return again

    def reduce_last(kind, again):
        wait_for(again)
        ends = []
        for blk in range(2):
            total = mid[kind, blk, y if blk == 0 else x].astype(f32)
            for step in range(SIDE - 1):
                total = total + rs2[kind, blk, step].astype(f32)
            ends.append(total.astype(bf16))
        return ends

    def send_home(kind, ends):
        rows = jnp.concatenate(ends, axis=0)
        out = product(unpack[0], rows[:, :LANES], 1, 0) + product(unpack[1], rows[:, LANES:], 1, 0)
        hsend[kind] = out.astype(bf16).reshape(GROUP, 16, LANES)
        hrecv[kind, me] = hsend[kind, me]
        return [copies.start(hsend.at[kind, g], hrecv.at[kind, me], device) for g, device in others]

    got_w1.wait_recv()
    begin(0)
    wait_for(gather_last(1, second_s))
    got_w2.wait_recv()
    begin(1)
    shared = []
    for j in range(2):
        value, grade = gelu_parts(whole(0, j))
        act[mine[j]] = value.astype(bf16)
        shared.append(copies.start(act.at[mine[j]], act.at[mine[j]], core))
        slope[j] = grade
    wait_for(shared)
    spread(0, act, w2, wx2, 0)
    sent_d = [
        copies.start(parts_out.at[(dp + step) % GROUP], parts_in.at[step - 1], peer) for step, peer in enumerate(peers, 1)
    ]
    found_out = reduce_first(0)
    active = act[...].reshape(SIDE * CHUNK, UNITS)
    gds[...] = product(active, ag[1, 1].reshape(SIDE * CHUNK, WIDTH), 0, 0).astype(bf16)
    got_gd = copies.start(gds, gdr, over)
    gd_own[...] = product(active, ag[1, 0].reshape(SIDE * CHUNK, WIDTH), 0, 0)

    wait_for(sent_d)
    total = parts_out[dp]
    for step in range(GROUP - 1):
        total = total + parts_in[step]
    dot_send[...] = total
    dot_home[me] = total
    sent_d = [copies.start(dot_send, dot_home.at[me], device) for _, device in others]
    shared = []
    for j in range(2):
        gh[mine[j]] = (whole(1, j) * slope[j]).astype(bf16)
        shared.append(copies.start(gh.at[mine[j]], gh.at[mine[j]], core))
        spread(1, gh, w1, wx1, 1, (mine[j],))
    for j in range(2):
        shared[j].wait_recv()
        spread(1, gh, w1, wx1, 1, (theirs[j],))
    found_in = reduce_first(1)
    again_out = reduce_second(0, found_out)
    grads = gh[...].reshape(SIDE * CHUNK, UNITS)
    gus[...] = product(nrm[1].reshape(SIDE * CHUNK, WIDTH), grads, 0, 0).astype(bf16)
    got_gu = copies.start(gus, gur, over)
    gu_own[...] = product(nrm[0].reshape(SIDE * CHUNK, WIDTH), grads, 0, 0)

    wait_for(sent_d)
    dots = jnp.zeros((8, LANES), f32)
    for expert in range(4):
        total = (dot_home[4 * expert] + dot_home[4 * expert + 1]) + (dot_home[4 * expert + 2] + dot_home[4 * expert + 3])
        dots = dots + jnp.where(iota((8, LANES), 0) == expert, total, 0.0)
    chooser = one_hot((line == me * CAP + (lane & 3)) & ((lane & 3) < CAP))
    dots_high = dots.astype(bf16)
    dots_low = (dots - dots_high.astype(f32)).astype(bf16)
    chosen = product(dots_high, chooser, 1, 0) + product(dots_low, chooser, 1, 0)
    chosen = summed(jnp.where(iota((8, LANES), 0) == (iota((8, LANES), 1) >> 2), chosen, 0.0))
    dot_first = jnp.sum(place_first.astype(f32) * chosen, axis=1, keepdims=True)
    dot_second = jnp.sum(place_second.astype(f32) * chosen, axis=1, keepdims=True)
    gap_grad = dot_first * gate_second - dot_second * gate_first
    normal = (normed[...] * gain_all + bias_all).astype(bf16)
    local = product(normal, (gap_grad * signed).astype(bf16), 0, 0).astype(bf16)
    for block_id in range(GROUP):
        for side in range(2):
            for path in range(2):
                begin_row = 128 * block_id + 64 * side + 32 * path
                lr[side, path, block_id // SIDE, block_id % SIDE] = local[begin_row:begin_row + 32]
    cored = copies.start(lr.at[1 - c], lc, core)

    base_value = gap_grad * product(signed.astype(bf16), rt[...], 1, 1)
    base[...] = base_value
    dense = two_rows(summed(base_value * normed[...]), summed(base_value))
    for block_id in range(GROUP):
        gb[block_id] = dense[:, 128 * block_id:128 * (block_id + 1)]
    for blk in range(2):
        gains = sum(pair_[0] for pair_ in sums[blk])
        biases = sum(pair_[1] for pair_ in sums[blk])
        dense = two_rows(gains, biases)
        for i in range(2):
            gb[spots[blk] + i] = gb[spots[blk] + i] + dense[:, LANES * i:LANES * (i + 1)]
    cored.wait_recv()
    l0[...] = (lr[c].astype(f32) + lc[...].astype(f32)).astype(bf16)
    sent_l = []
    for step in range(1, SIDE):
        sent_l.append(copies.start(l0.at[0, (x + step) % SIDE], l1.at[0, step - 1], along_x[step - 1]))
        sent_l.append(copies.start(l0.at[1, :, (y + step) % SIDE], l1.at[1, step - 1], along_y[step - 1]))
    sent_g = [
        copies.start(gb.at[(dp + step) % GROUP], gbr.at[step - 1], peer) for step, peer in enumerate(peers, 1)
    ]
    again_in = reduce_second(1, found_in)
    home_out = send_home(0, reduce_last(0, again_out))
    wait_for(sent_l)
    for path in range(2):
        own_part = l0[0, x] if path == 0 else l0[1, :, y]
        l2[path] = (
            own_part.astype(f32) + l1[path, 0].astype(f32) + l1[path, 1].astype(f32) + l1[path, 2].astype(f32)
        ).astype(bf16)
    sent_l = []
    for step in range(1, SIDE):
        sent_l.append(copies.start(l2.at[0, (y + step) % SIDE], l3.at[0, step - 1], along_y[step - 1]))
        sent_l.append(copies.start(l2.at[1, (x + step) % SIDE], l3.at[1, step - 1], along_x[step - 1]))
    home_in = send_home(1, reduce_last(1, again_in))
    wait_for(sent_g)
    total = gb[dp]
    for step in range(GROUP - 1):
        total = total + gbr[step]
    gb1[...] = total
    gb2[2 * inner + c] = total
    sent_g = [copies.start(gb1, gb2.at[2 * inner + c], device) for device in octet]
    wait_for(sent_l)
    for path in range(2):
        own_part = l2[path, y if path == 0 else x]
        total = (own_part.astype(f32) + l3[path, 0].astype(f32)) + (l3[path, 1].astype(f32) + l3[path, 2].astype(f32))
        l4[2 * path] = total[0:16].astype(bf16)
        l4[2 * path + 1] = total[16:32].astype(bf16)
    sent_l = [copies.start(l4.at[(inner + step) % 4], l5.at[step - 1], along_in[step - 1]) for step in range(1, 4)]
    wait_for(sent_g)
    total = gb2[0]
    for i in range(1, 8):
        total = total + gb2[i]
    gb3[outer] = total
    sent_g = [copies.start(gb3.at[outer], gb3.at[outer], device) for device in along_out]
    wait_for(sent_l)
    l6[...] = (
        (l4[inner].astype(f32) + l5[0].astype(f32)) + (l5[1].astype(f32) + l5[2].astype(f32))
    ).astype(bf16)
    sent_l = [copies.start(l6, l7.at[outer], device) for device in along_out]
    l7[outer] = l6[...]

    wait_for(home_out)
    rows = returned(0)
    moe_out[...] = (
        gate_first * product(place_first, rows, 1, 0) + gate_second * product(place_second, rows, 1, 0)
    ).astype(bf16)
    wait_for(home_in)
    grad_norm = (product(place_all, returned(1), 1, 0) + base[...]) * gain_all
    mean_grad = jnp.mean(grad_norm, axis=1, keepdims=True)
    mean_both = jnp.mean(grad_norm * normed[...], axis=1, keepdims=True)
    grad_in[...] = (scale_inv * (grad_norm - mean_grad - normed[...] * mean_both)).astype(bf16)
    wait_for(sent_l)
    fin[c, inner] = (
        (l7[0].astype(f32) + l7[1].astype(f32)) + (l7[2].astype(f32) + l7[3].astype(f32))
    ).astype(bf16)
    sent_l = [copies.start(fin.at[c, inner], fin.at[c, inner], device) for device in octet]
    got_gd.wait_recv()
    gd_out[...] = (gd_own[...] + gdr[...].astype(f32)).astype(bf16)
    got_gu.wait_recv()
    gu_out[...] = (gu_own[...] + gur[...].astype(f32)).astype(bf16)
    wait_for(sent_g)
    total = (gb3[0] + gb3[1]) + (gb3[2] + gb3[3])
    gain_out[...] = total[0:1]
    bias_out[...] = total[1:2]
    wait_for(sent_l)
    router_out[...] = fin[...].astype(f32).reshape(128, 128)
    copies.finish()


def last_kernel(*refs):
    count = len(refs) // 2
    for i in range(count):
        refs[count + i][...] = refs[i][...]


def on_device(tokens, cotangent, routes, ln_gain, ln_bias, router_weight, up_weight, down_weight):
    vmem = pl.BlockSpec(memory_space=pltpu.VMEM)
    pair = (2, 2, CHUNK, UNITS)
    moved = (2, 2, SIDE, SIDE, ROWS, WIDTH)
    dense = (8, LANES)
    scratch = [
        ((TOKENS, HIDDEN), f32),
        ((2, 80, LANES), bf16),
        ((2, GROUP, 80, LANES), bf16),
        ((HIDDEN, LANES), bf16),
        ((2, GROUP, 16, LANES), bf16),
        ((2, GROUP, 16, LANES), bf16),
        (moved, bf16),
        ((WIDTH, UNITS), bf16),
        ((UNITS, WIDTH), bf16),
        (pair, f32),
        (pair, bf16),
        (pair, bf16),
        (pair, bf16),
        (pair, bf16),
        ((SIDE, CHUNK, UNITS), bf16),
        ((SIDE, CHUNK, UNITS), bf16),
        ((2, CHUNK, UNITS), f32),
        (moved, bf16),
        ((2, 2, SIDE - 1, SIDE, ROWS, WIDTH), bf16),
        ((2, 2, SIDE, ROWS, WIDTH), bf16),
        ((2, 2, SIDE - 1, ROWS, WIDTH), bf16),
        ((2, GROUP, 16, LANES), bf16),
        ((2, GROUP, 16, LANES), bf16),
        ((UNITS, WIDTH), bf16),
        ((UNITS, WIDTH), bf16),
        ((WIDTH, UNITS), bf16),
        ((WIDTH, UNITS), bf16),
        ((UNITS, WIDTH), f32),
        ((WIDTH, UNITS), f32),
        ((TOKENS, HIDDEN), f32),
        ((2, 2, SIDE, SIDE, 32, LANES), bf16),
        ((2, SIDE, SIDE, 32, LANES), bf16),
        ((2, SIDE, SIDE, 32, LANES), bf16),
        ((2, SIDE - 1, SIDE, 32, LANES), bf16),
        ((2, SIDE, 32, LANES), bf16),
        ((2, SIDE - 1, 32, LANES), bf16),
        ((4, 16, LANES), bf16),
        ((3, 16, LANES), bf16),
        ((16, LANES), bf16),
        ((4, 16, LANES), bf16),
        ((2, 4, 16, LANES), bf16),
        ((2, SIDE, CHUNK, WIDTH), bf16),
        ((GROUP,) + dense, f32),
        ((GROUP - 1,) + dense, f32),
        (dense, f32),
        ((8,) + dense, f32),
        ((4,) + dense, f32),
        ((GROUP,) + dense, f32),
        ((GROUP - 1,) + dense, f32),
        (dense, f32),
        ((GROUP,) + dense, f32),
    ]
    count = 256
    found = pl.pallas_call(
        step_kernel,
        out_shape=[
            jax.ShapeDtypeStruct(tokens.shape, bf16),
            jax.ShapeDtypeStruct(tokens.shape, bf16),
            jax.ShapeDtypeStruct((WIDTH, UNITS), bf16),
            jax.ShapeDtypeStruct((UNITS, WIDTH), bf16),
            jax.ShapeDtypeStruct((128, LANES), f32),
            jax.ShapeDtypeStruct((1, LANES), f32),
            jax.ShapeDtypeStruct((1, LANES), f32),
        ],
        in_specs=[vmem] * 8,
        out_specs=[vmem] * 7,
        scratch_shapes=[pltpu.VMEM(shape, kind) for shape, kind in scratch]
        + [pltpu.SemaphoreType.DMA((count,)), pltpu.SemaphoreType.DMA((count,))],
        compiler_params=pltpu.CompilerParams(collective_id=0, has_side_effects=True, vmem_limit_bytes=56 << 20),
    )(tokens, cotangent, routes.T, ln_gain[None], ln_bias[None], router_weight, up_weight[0], down_weight[0])
    moe_out, grad_input, grad_up, grad_down, grad_router, grad_gain, grad_bias = pl.pallas_call(
        last_kernel,
        out_shape=[jax.ShapeDtypeStruct(array.shape, array.dtype) for array in found],
        in_specs=[vmem] * 7,
        out_specs=[vmem] * 7,
        compiler_params=pltpu.CompilerParams(vmem_limit_bytes=60 << 20),
    )(*found)
    return (moe_out, grad_input, grad_up[None], grad_down[None], grad_router, grad_gain[0], grad_bias[0])


def solution(mesh):
    return jax.shard_map(
        on_device,
        mesh=mesh,
        in_specs=(
            P(("dp", "expert"), None),
            P(("dp", "expert"), None),
            P(("dp", "expert"), None),
            P("dp"),
            P("dp"),
            P("dp", None),
            P("expert", None, "dp"),
            P("expert", "dp", None),
        ),
        out_specs=(
            P(("dp", "expert"), None),
            P(("dp", "expert"), None),
            P("expert", None, "dp"),
            P("expert", "dp", None),
            P("dp", None),
            P("dp"),
            P("dp"),
        ),
        check_vma=False,
    )
```

time: 135 us -> 121 us (0.90)
  local copies, waits for them, and re-layouts: 8.26 us -> 0 us
  Pallas kernels: 126 us -> 120 us
    pallas_call x1, Pallas kernels: 126 us -> 118 us  [on_device(): pl.pallas_call(step_kernel, out_shape=[jax.ShapeDtypeStruct(tokens.shape,...]
    unnamed x14 -> x0, local copies, waits for them, and re-layouts: 6.98 us -> none
    pallas_call x0 -> x1, Pallas kernels: none -> 2.54 us  [on_device(): pl.pallas_call(last_kernel, out_shape=[jax.ShapeDtypeStruct(array.shape,...]
where the time goes in v3:
time: 121 us
  Pallas kernels  120 us (99%)
    pallas_call x1, Pallas kernels, on_device(): pl.pallas_call(step_kernel, out_shape=[jax.ShapeDtypeStruct(tokens.shape,...  118 us
    pallas_call x1, Pallas kernels, on_device(): pl.pallas_call(last_kernel, out_shape=[jax.ShapeDtypeStruct(array.shape,...  2.54 us

profile of v3, /device:TPU:1, one launch (start us, length us, event | category | flops | bytes accessed | tf_op | source)
XLA Modules:
  0.0 121.0 jit_solution(10978539980148681127)
XLA Ops:
  0.6 117.8 %shard_map.135 = (bf16[128,2048]{1,0:T(8,128)(2,1)}, bf16[128,2048]{1,0:T(8,128)(2,1)}, bf16[256,512]{1,0:T(8,128)(2,1)}, bf16[512,256]{1,0:T(8,128)(2,1)}, f32[...) custom-call(bf16[128,2048]{1,0:T(8,128)(2,1)} %tokens.1, bf16[128,2048]{1,0:T(8,128)(2,1)} %cot.1, ...), custom_call_target="tpu_custom_call" | custom-call | tf_op jit(solution)/shard_map/pallas_call | solution.py:603
  118.4 2.5 %shard_map.136 = (bf16[128,2048]{1,0:T(8,128)(2,1)}, bf16[128,2048]{1,0:T(8,128)(2,1)}, bf16[256,512]{1,0:T(8,128)(2,1)}, bf16[512,256]{1,0:T(8,128)(2,1)}, f32[...) custom-call(bf16[128,2048]{1,0:T(8,128)(2,1)} %get-tuple-element.21.refs_0_, ...), custom_call_target="tpu_custom_call" | custom-call | tf_op jit(solution)/shard_map/pallas_call | solution.py:620

commit v4 on v3

--- a/solution.py
+++ b/solution.py
@@ -400,7 +400,6 @@
     found_out = reduce_first(0)
     active = act[...].reshape(SIDE * CHUNK, UNITS)
     gds[...] = product(active, ag[1, 1].reshape(SIDE * CHUNK, WIDTH), 0, 0).astype(bf16)
-    got_gd = copies.start(gds, gdr, over)
     gd_own[...] = product(active, ag[1, 0].reshape(SIDE * CHUNK, WIDTH), 0, 0)
 
     wait_for(sent_d)
@@ -415,6 +414,7 @@
         gh[mine[j]] = (whole(1, j) * slope[j]).astype(bf16)
         shared.append(copies.start(gh.at[mine[j]], gh.at[mine[j]], core))
         spread(1, gh, w1, wx1, 1, (mine[j],))
+    got_gd = copies.start(gds, gdr, over)
     for j in range(2):
         shared[j].wait_recv()
         spread(1, gh, w1, wx1, 1, (theirs[j],))
@@ -507,6 +507,11 @@
     sent_l = [copies.start(l6, l7.at[outer], device) for device in along_out]
     l7[outer] = l6[...]
 
+    wait_for(sent_l)
+    fin[c, inner] = (
+        (l7[0].astype(f32) + l7[1].astype(f32)) + (l7[2].astype(f32) + l7[3].astype(f32))
+    ).astype(bf16)
+    sent_l = [copies.start(fin.at[c, inner], fin.at[c, inner], device) for device in octet]
     wait_for(home_out)
     rows = returned(0)
     moe_out[...] = (
@@ -517,11 +522,6 @@
     mean_grad = jnp.mean(grad_norm, axis=1, keepdims=True)
     mean_both = jnp.mean(grad_norm * normed[...], axis=1, keepdims=True)
     grad_in[...] = (scale_inv * (grad_norm - mean_grad - normed[...] * mean_both)).astype(bf16)
-    wait_for(sent_l)
-    fin[c, inner] = (
-        (l7[0].astype(f32) + l7[1].astype(f32)) + (l7[2].astype(f32) + l7[3].astype(f32))
-    ).astype(bf16)
-    sent_l = [copies.start(fin.at[c, inner], fin.at[c, inner], device) for device in octet]
     got_gd.wait_recv()
     gd_out[...] = (gd_own[...] + gdr[...].astype(f32)).astype(bf16)
     got_gu.wait_recv()

time: 121 us -> 121 us (level)
  no operation moved by 1% of the time
where the time goes in v4:
time: 121 us
  Pallas kernels  120 us (99%)
    pallas_call x1, Pallas kernels, on_device(): pl.pallas_call(step_kernel, out_shape=[jax.ShapeDtypeStruct(tokens.shape,...  117 us
    pallas_call x1, Pallas kernels, on_device(): pl.pallas_call(last_kernel, out_shape=[jax.ShapeDtypeStruct(array.shape,...  2.54 us

profile of v4, /device:TPU:1, one launch (start us, length us, event | category | flops | bytes accessed | tf_op | source)
XLA Modules:
  0.0 120.5 jit_solution(6252998699162025355)
XLA Ops:
  0.6 117.3 %shard_map.135 = (bf16[128,2048]{1,0:T(8,128)(2,1)}, bf16[128,2048]{1,0:T(8,128)(2,1)}, bf16[256,512]{1,0:T(8,128)(2,1)}, bf16[512,256]{1,0:T(8,128)(2,1)}, f32[...) custom-call(bf16[128,2048]{1,0:T(8,128)(2,1)} %tokens.1, bf16[128,2048]{1,0:T(8,128)(2,1)} %cot.1, ...), custom_call_target="tpu_custom_call" | custom-call | tf_op jit(solution)/shard_map/pallas_call | solution.py:603
  118.0 2.5 %shard_map.136 = (bf16[128,2048]{1,0:T(8,128)(2,1)}, bf16[128,2048]{1,0:T(8,128)(2,1)}, bf16[256,512]{1,0:T(8,128)(2,1)}, bf16[512,256]{1,0:T(8,128)(2,1)}, f32[...) custom-call(bf16[128,2048]{1,0:T(8,128)(2,1)} %get-tuple-element.21.refs_0_, ...), custom_call_target="tpu_custom_call" | custom-call | tf_op jit(solution)/shard_map/pallas_call | solution.py:620
